TPU v7x, 768 devices: a whole 4x8x12 slice. The times are simulated.
768 devices in a mesh: grp: 8 (over y), own: 8 (over x, core), rep: 12 (over z).
Axes of the slice: x: 4, y: 8, z: 12, core: 2. Of those that a mesh axis runs over, the one named last changes fastest.
Arguments:
- self_feat: bfloat16 [786432, 256], P(('grp', 'own', 'rep')), may hold values from -6 to 6
- neighbor: int32 [786432, 15], P(('grp', 'own', 'rep')), may hold values from 0 to 2815
- grad_out: bfloat16 [786432, 256], P(('grp', 'own', 'rep')), may hold values from -0.015625 to 0.015625
- fetch_rows: int32 [6144, 96], P(('grp', 'own', 'rep')), may hold values from 0 to 4095
- fetch_count: int32 [6144], P(('grp', 'own', 'rep')), may hold values from 12 to 96, as said below
- table_codes: bfloat16 [32768, 256], P('own'), may hold values from -6 to 6
- table_scale: bfloat16 [32768, 2], P('own'), may hold values from 0.5 to 2
- hot_table: bfloat16 [2048, 256], replicated, may hold values from -6 to 6
- self_weight: bfloat16 [256, 256], replicated, may hold values from -0.375 to 0.375
- neighbor_weight: bfloat16 [256, 256], replicated, may hold values from -0.375 to 0.375
Outputs:
- hidden: bfloat16 [786432, 256], P(('grp', 'own', 'rep'))
- self_grad: float32 [256, 256], replicated
- neighbor_grad: float32 [256, 256], replicated
Inputs may be any that keep to these rules, and one draw needn't show every extreme that they name: `fetch_count`: in every group of devices sharing grp and rep indices, one owner is asked for exactly 96 rows by every device of the group; other counts lie from 12 to 48.
All inputs are finite; a program needn't handle non-finite values.
Results may differ from a plain program's by a relative error of at most 0.0056.
Values may be sent and summed in bfloat16 or wider, within the bound.
No kernel may reach another device: no remote copies, remote signals or barrier semaphores. Data moves between devices by JAX's collectives and lax.ppermute only.
A program may use at most 128 MiB of HBM per device.

v0:
```python
import jax
import jax.numpy as jnp
from jax import lax
from jax.sharding import PartitionSpec as P


def silu_slope(value):
    sigma = jax.nn.sigmoid(value)
    return sigma * (1.0 + value * (1.0 - sigma))


def body(
    self_feat,
    neighbor,
    grad_out,
    fetch_rows,
    fetch_count,
    table_codes,
    table_scale,
    hot_table,
    self_weight,
    neighbor_weight,
):
    owners = lax.axis_size("own")
    slots = fetch_rows.shape[1]
    width = table_codes.shape[1]
    blocks = table_scale.shape[1]
    hot_rows = hot_table.shape[0]
    wanted = lax.all_to_all(fetch_rows, "own", split_axis=0, concat_axis=0, tiled=True)
    found_codes = table_codes[wanted]
    found_scales = table_scale[wanted]
    code_rows = lax.all_to_all(found_codes, "own", split_axis=0, concat_axis=0, tiled=True)
    scales = lax.all_to_all(found_scales, "own", split_axis=0, concat_axis=0, tiled=True)
    decoded = (
        code_rows.reshape(owners, slots, blocks, width // blocks).astype(jnp.float32)
        * scales.astype(jnp.float32)[:, :, :, None]
    )
    slot_live = jnp.arange(slots, dtype=jnp.int32)[None, :] < fetch_count[:, None]
    decoded = decoded.reshape(owners, slots, width)
    cold_rows = jnp.where(slot_live[:, :, None], decoded, jnp.zeros_like(decoded)).astype(
        jnp.bfloat16
    )
    pool_rows = jnp.concatenate([hot_table, cold_rows.reshape(owners * slots, width)], axis=0)
    pool_live = jnp.concatenate(
        [jnp.ones((hot_rows,), jnp.int32), slot_live.reshape(-1).astype(jnp.int32)]
    )
    picked = pool_rows[neighbor]
    summed = self_feat.astype(jnp.float32) + jnp.sum(picked, axis=1, dtype=jnp.float32)
    divisor = (1 + jnp.sum(pool_live[neighbor], axis=1)).astype(jnp.float32)
    mean_feat = (summed / divisor[:, None]).astype(jnp.bfloat16)
    preact = jnp.dot(self_feat, self_weight, preferred_element_type=jnp.float32) + jnp.dot(
        mean_feat, neighbor_weight, preferred_element_type=jnp.float32
    )
    hidden = jax.nn.silu(preact).astype(jnp.bfloat16)
    delta = (grad_out.astype(jnp.float32) * silu_slope(preact)).astype(jnp.bfloat16)
    grad_self = jnp.dot(self_feat.T, delta, preferred_element_type=jnp.float32)
    grad_nbr = jnp.dot(mean_feat.T, delta, preferred_element_type=jnp.float32)
    grad_self, grad_nbr = lax.psum((grad_self, grad_nbr), ("grp", "own", "rep"))
    return (hidden, grad_self, grad_nbr)


def solution(mesh):
    in_specs = (
        P(("grp", "own", "rep"), None),
        P(("grp", "own", "rep"), None),
        P(("grp", "own", "rep"), None),
        P(("grp", "own", "rep"), None),
        P(("grp", "own", "rep")),
        P("own", None),
        P("own", None),
        P(),
        P(),
        P(),
    )
    out_specs = (P(("grp", "own", "rep"), None), P(), P())
    return jax.shard_map(body, mesh=mesh, in_specs=in_specs, out_specs=out_specs, check_vma=False)
```

profile of v0, /device:TPU:1, one launch (start us, length us, event | category | flops | bytes accessed | tf_op | source)
XLA Modules:
  0.0 707.4 jit_solution(14662957270592721485)
XLA Ops:
  7.2 13.9 %all-to-all-start = ((s32[8,1,96]{2,1,0:T(1,128)}), s32[8,1,96]{2,1,0:T(1,128)S(1)}, u32[]{:S(2)}, u32[]{:S(2)}) async-start(s32[8,1,96]{2,1,0:T(1,128)} %bitcast.20), calls=%async_computation | async-start | bytes 8192 | tf_op jit(solution)/shard_map/all_to_all | solution.py:29
  21.1 0.8 compare_select_fusion
  21.9 0.2 copy.27
  22.1 0.3 reshape.93
  22.5 2.4 fusion
  25.0 0.5 copy.23
  25.5 0.1 convert_element_type.44
  25.7 1.9 gather_fusion.1
  27.6 0.7 copy.24
  28.3 4.8 all-to-all-start.2
  33.2 84.9 %gather_fusion.3 = s32[15360]{0:T(1024)S(1)} fusion(s32[2816]{0:T(1024)S(1)} %pad_convert_fusion, s32[15360]{0:T(1024)S(1)} %broadcast_clamp_fusion), kind=kCustom, calls=%fused_computation.3 | custom fusion | bytes 184320 | tf_op jit(solution)/shard_map/gather | solution.py:49
  118.1 0.4 reshape.104
  118.5 0.2 reduce_sum.19
  118.7 3.4 gather_fusion
  122.1 4.8 all-to-all-start.1
  126.9 0.7 copy_convert_fusion
  127.6 0.9 copy.26
  128.6 1.9 mul.24
  130.5 1.5 mul.25
  132.0 3.0 all-to-all-done.1
  135.0 1.3 select_convert_fusion
  136.3 1.3 pad_maximum_fusion
  137.6 65.8 %gather_fusion.2 = bf16[15360,256]{1,0:T(8,128)(2,1)} fusion(bf16[2816,256]{1,0:T(8,128)(2,1)S(1)} %pad_maximum_fusion, s32[15360]{0:T(1024)} %copy-done.1), kind=kCustom, calls=%fused_computation.2 | custom fusion | bytes 15790080 | tf_op jit(solution)/shard_map/gather | solution.py:47
  203.5 12.9 %reshape.113 = f32[1024,15,256]{2,1,0:T(8,128)} reshape(bf16[15360,256]{1,0:T(8,128)(2,1)} %gather_fusion.2) | data formatting | bytes 23592960 | tf_op jit(solution)/shard_map/convert_element_type | solution.py:48
  216.4 9.9 %reduce_sum.18 = f32[1024,256]{1,0:T(8,128)} reduce(f32[1024,15,256]{2,1,0:T(8,128)} %reshape.113, f32[]{:T(128)} %constant.9.clone.1), dimensions={1}, to_apply=%region_0.1 | reduce | flops 3670016 | bytes 16777220 | tf_op jit(solution)/shard_map/reduce_sum | solution.py:48
  226.2 1.4 divide_convert_fusion
  227.7 2.7 multiply_convert_fusion
  230.3 1.0 fusion.1
  231.4 1.0 convolution_bitcast_fusion
  232.5 464.6 %all-reduce.4.cloned.1.call-done = (f32[256,256]{0,1:T(8,128)}, f32[256,256]{1,0:T(8,128)}) async-done(((f32[256,256]{0,1:T(8,128)}, f32[256,256]{1,0:T(8,128)}), (f32[256,256]{0,1:T(8,128)}, f32[256,256]{1,0:T(8,128)})) %all-reduce.4.cloned.1.call-update) | async-done | bytes 524304 | tf_op jit(solution)/shard_map/psum | solution.py:58
  697.1 1.8 copy.28
  698.8 1.7 copy.32
  (31 shorter events, 0.3 us)
Async XLA Ops:
  7.2 111.5 %copy-start = (bf16[4096,256]{1,0:T(8,128)(2,1)S(1)}, bf16[4096,256]{1,0:T(8,128)(2,1)}, u32[]{:S(2)}) copy-start(bf16[4096,256]{1,0:T(8,128)(2,1)} %param.15) | copy-start | bytes 6291460
  7.2 17.8 %copy-start.9 = (s32[8]{0:T(128)S(1)}, s32[8]{0:T(128)}, u32[]{:S(2)}) copy-start(s32[8]{0:T(128)} %param.14) | copy-start | bytes 100
  7.2 17.8 %copy-start.4 = (bf16[4096,2]{0,1:T(2,128)(2,1)S(1)}, bf16[4096,2]{0,1:T(2,128)(2,1)}, u32[]{:S(2)}) copy-start(bf16[4096,2]{0,1:T(2,128)(2,1)} %param.16) | copy-start | bytes 49156
  7.2 18.4 %all-to-all-start = ((s32[8,1,96]{2,1,0:T(1,128)}), s32[8,1,96]{2,1,0:T(1,128)S(1)}, u32[]{:S(2)}, u32[]{:S(2)}) async-start(s32[8,1,96]{2,1,0:T(1,128)} %bitcast.20), calls=%async_computation | async-start | bytes 8192 | tf_op jit(solution)/shard_map/all_to_all | solution.py:29
  22.5 95.6 %copy-start.1 = (s32[15360]{0:T(1024)}, s32[15360]{0:T(1024)S(1)}, u32[]{:S(2)}) copy-start(s32[15360]{0:T(1024)S(1)} %broadcast_clamp_fusion) | copy-start | bytes 184324
  25.0 0.7 copy-start.5
  25.7 92.4 %copy-start.3 = (s32[1024]{0:T(1024)}, s32[1024]{0:T(1024)S(1)}, u32[]{:S(2)}) copy-start(s32[1024]{0:T(1024)S(1)} %pad_clamp_fusion) | copy-start | bytes 12292
  28.3 93.8 %all-to-all-start.2 = ((bf16[8,96,2]{1,2,0:T(2,128)(2,1)}), bf16[8,96,2]{1,2,0:T(2,128)(2,1)}, u32[]{:S(2)}, u32[]{:S(2)}) async-start(bf16[8,96,2]{1,2,0:T(2,128)(2,1)} %copy.24), calls=%async_computation.2 | async-start | bytes 8192 | tf_op jit(solution)/shard_map/all_to_all | solution.py:33
  118.7 16.3 %copy-start.6 = (pred[8,96]{1,0:T(8,128)(4,1)S(1)}, pred[8,96]{1,0:T(8,128)(4,1)}, u32[]{:S(2)}) copy-start(pred[8,96]{1,0:T(8,128)(4,1)} %copy-done.5) | copy-start | bytes 2308
  122.1 12.9 %all-to-all-start.1 = ((bf16[8,96,256]{2,1,0:T(8,128)(2,1)}), bf16[8,96,256]{2,1,0:T(8,128)(2,1)S(1)}, u32[]{:S(2)}, u32[]{:S(2)}) async-start(bf16[8,96,256]{2,1,0:T(8,128)(2,1)} %bitcast.2), calls=%async_computation.1 | async-start | bytes 786432 | tf_op jit(solution)/shard_map/all_to_all | solution.py:32
  126.9 570.1 %all-reduce.4.cloned.1.call-start = ((), (), s32[]{:S(2)}) async-start(), calls=%async_computation.3 | async-start | bytes 1048576 | tf_op jit(solution)/shard_map/psum | solution.py:58
  216.4 9.9 %copy-start.2 = (bf16[1024,256]{1,0:T(8,128)(2,1)S(1)}, bf16[1024,256]{1,0:T(8,128)(2,1)}, u32[]{:S(2)}) copy-start(bf16[1024,256]{1,0:T(8,128)(2,1)} %param.10) | copy-start | bytes 1572868
  216.4 11.3 %copy-start.7 = (bf16[1024,256]{1,0:T(8,128)(2,1)S(1)}, bf16[1024,256]{1,0:T(8,128)(2,1)}, u32[]{:S(2)}) copy-start(bf16[1024,256]{1,0:T(8,128)(2,1)} %param.12) | copy-start | bytes 1572868
  216.4 11.3 %copy-start.8 = (bf16[256,256]{1,0:T(8,128)(2,1)S(1)}, bf16[256,256]{1,0:T(8,128)(2,1)}, u32[]{:S(2)}) copy-start(bf16[256,256]{1,0:T(8,128)(2,1)} %param.19) | copy-start | bytes 393220
Sparse Core Ops, SparseCore 0:
  232.6 464.4 all-reduce.3
where the time goes:
time: 710 us; the launch traced here: 707 us
  waiting for transfers between devices  468 us (66%)
  local copies, waits for them, and re-layouts  179 us (25%)
  starting transfers between devices  23.5 us (3%)
  other arithmetic  15.7 us (2%)
  between operations  14.2 us (2%)
  matrix products  7.18 us (1%)
    psum x1, waiting for transfers between devices, body(): grad_self, grad_nbr = lax.psum((grad_self, grad_nbr), ('grp', 'own', 'rep'))  465 us
    gather x2, local copies, waits for them, and re-layouts, body(): divisor = (1 + jnp.sum(pool_live[neighbor], axis=1)).astype(jnp.float32)  85.3 us
    gather x1, local copies, waits for them, and re-layouts, body(): picked = pool_rows[neighbor]  65.8 us
  transfers between devices with their start and end apart: 4, of which 2 were waited for; matrix products, arithmetic and copies ran while one was open for 14% of the time, Pallas kernels for 0%

commit v1 on v0

v1 whole, which is shorter than its diff:
```python
import jax
import jax.numpy as jnp
from jax import lax
from jax.experimental import pallas as pl
from jax.experimental.pallas import tpu as pltpu
from jax.sharding import PartitionSpec as P

F32 = jnp.float32
BF16 = jnp.bfloat16
LANES = 128
STEP = 16


def count_kernel(nbr_ref, self_ref, hot_ref, sum_ref, cold_ref, cols_ref, counts_ref):
    neighbors, targets = nbr_ref.shape
    hot_blocks = hot_ref.shape[0] // LANES
    cold_blocks = cold_ref.shape[1] // LANES
    blocks = hot_blocks + cold_blocks
    groups = (blocks + 7) // 8
    rows = nbr_ref[...]
    pad = jnp.zeros((16 - neighbors, targets), jnp.int32)
    cols_ref[...] = jnp.concatenate([rows, pad], axis=0).T
    lane = lax.broadcasted_iota(jnp.int32, (STEP, LANES), 1)

    def step(i, carry):
        at = pl.ds(pl.multiple_of(i * STEP, STEP), STEP)
        own = cols_ref[at, :]
        words = [jnp.zeros((STEP, LANES), jnp.int32) for _ in range(groups)]
        for k in range(neighbors):
            row = jnp.broadcast_to(own[:, k : k + 1], (STEP, LANES))
            bit = jnp.left_shift(jnp.int32(1), jnp.bitwise_and(jnp.right_shift(row, 5), 28))
            key = jnp.bitwise_and(row, ~0x380)
            for g in range(groups):
                words[g] = words[g] + jnp.where(key == lane + g * 1024, bit, 0)
        for b in range(blocks):
            word = words[b // 8]
            if b % 8:
                word = lax.shift_right_logical(word, 4 * (b % 8))
            count = jnp.bitwise_and(word, 15).astype(F32).astype(BF16)
            if b < hot_blocks:
                counts_ref[at, b * LANES : (b + 1) * LANES] = count
            else:
                c = b - hot_blocks
                cold_ref[at, c * LANES : (c + 1) * LANES] = count
        return carry

    lax.fori_loop(0, targets // STEP, step, 0, unroll=2)
    sum_ref[...] = self_ref[...].astype(F32) + jnp.dot(
        counts_ref[...], hot_ref[...], preferred_element_type=F32
    )


def decode_kernel(code_ref, scale_ref, out_ref):
    blocks = scale_ref.shape[0]
    width = code_ref.shape[1]
    which = lax.broadcasted_iota(jnp.int32, (blocks, width), 0)
    block = lax.broadcasted_iota(jnp.int32, (blocks, width), 1) // (width // blocks)
    ones = jnp.where(which == block, 1.0, 0.0).astype(BF16)
    scale = lax.dot_general(
        scale_ref[...], ones, (((0,), (0,)), ((), ())), preferred_element_type=F32
    )
    out_ref[...] = (code_ref[...].astype(F32) * scale).astype(BF16)


def select_kernel(want_ref, table_ref, out_ref, cols_ref):
    peers, slots = want_ref.shape
    rows = table_ref.shape[0]
    cols_ref[...] = want_ref[...].T
    lane = lax.broadcasted_iota(jnp.int32, (slots, rows), 1)
    for p in range(peers):
        want = jnp.broadcast_to(cols_ref[:, p : p + 1], (slots, rows))
        pick = jnp.where(want == lane, 1.0, 0.0).astype(BF16)
        out_ref[p] = jnp.dot(pick, table_ref[...], preferred_element_type=F32).astype(BF16)


def layer_kernel(
    live_ref,
    sum_ref,
    counts_ref,
    rows_ref,
    self_ref,
    grad_ref,
    self_w_ref,
    nbr_w_ref,
    hidden_ref,
    grads_ref,
    cold_ref,
    dead_ref,
    total_ref,
):
    owners, slots, width = rows_ref.shape
    step = pl.program_id(0)

    @pl.when(step == 0)
    def _():
        for p in range(owners):
            at = slice(p * slots, (p + 1) * slots)
            slot = lax.broadcasted_iota(jnp.int32, (slots, width), 0)
            live = slot < live_ref[p]
            cold_ref[at, :] = jnp.where(live, rows_ref[p].astype(F32), 0.0).astype(BF16)
            dead_ref[at, :] = jnp.where(live[:, :LANES], 0.0, 1.0).astype(BF16)
        total_ref[...] = jnp.zeros_like(total_ref)

    counts = counts_ref[...]
    summed = sum_ref[...] + jnp.dot(counts, cold_ref[...], preferred_element_type=F32)
    dead = jnp.dot(counts, dead_ref[...], preferred_element_type=F32)
    share = 1.0 / (16.0 - dead)
    share = jnp.concatenate([share] * (width // LANES), axis=1)
    mean = (summed * share).astype(BF16)
    own = self_ref[...]
    pre = jnp.dot(own, self_w_ref[...], preferred_element_type=F32) + jnp.dot(
        mean, nbr_w_ref[...], preferred_element_type=F32
    )
    sigma = 1.0 / (1.0 + jnp.exp(-pre))
    hidden_ref[...] = (pre * sigma).astype(BF16)
    slope = sigma * (1.0 + pre * (1.0 - sigma))
    delta = (grad_ref[...].astype(F32) * slope).astype(BF16)
    across = (((0,), (0,)), ((), ()))
    total_ref[:width, :] += lax.dot_general(own, delta, across, preferred_element_type=F32)
    total_ref[width:, :] += lax.dot_general(mean, delta, across, preferred_element_type=F32)

    @pl.when(step == pl.num_programs(0) - 1)
    def _():
        grads_ref[...] = total_ref[...].astype(BF16)


def whole(shape):
    return pl.BlockSpec(shape, lambda i: (0,) * len(shape))


def count_rows(neighbor, self_feat, hot_table, cold):
    targets, width = self_feat.shape
    neighbors = neighbor.shape[1]
    hot = hot_table.shape[0]
    tile = 256
    return pl.pallas_call(
        count_kernel,
        grid=(targets // tile,),
        in_specs=[
            pl.BlockSpec((neighbors, tile), lambda i: (0, i)),
            pl.BlockSpec((tile, width), lambda i: (i, 0)),
            whole((hot, width)),
        ],
        out_specs=[
            pl.BlockSpec((tile, width), lambda i: (i, 0)),
            pl.BlockSpec((tile, cold), lambda i: (i, 0)),
        ],
        out_shape=[
            jax.ShapeDtypeStruct((targets, width), F32),
            jax.ShapeDtypeStruct((targets, cold), BF16),
        ],
        scratch_shapes=[pltpu.VMEM((tile, 16), jnp.int32), pltpu.VMEM((tile, hot), BF16)],
        cost_estimate=pl.CostEstimate(
            flops=2 * targets * hot * width, bytes_accessed=16 * 2**20, transcendentals=0
        ),
        compiler_params=pltpu.CompilerParams(vmem_limit_bytes=32 * 2**20),
        name="count_rows",
    )(neighbor.T, self_feat, hot_table)


def decode_table(codes, scale):
    rows, width = codes.shape
    blocks = scale.shape[1]
    tile = 1024
    return pl.pallas_call(
        decode_kernel,
        grid=(rows // tile,),
        in_specs=[
            pl.BlockSpec((tile, width), lambda i: (i, 0)),
            pl.BlockSpec((blocks, tile), lambda i: (0, i)),
        ],
        out_specs=pl.BlockSpec((tile, width), lambda i: (i, 0)),
        out_shape=jax.ShapeDtypeStruct((rows, width), BF16),
        cost_estimate=pl.CostEstimate(
            flops=2 * rows * width, bytes_accessed=4 * 2**20, transcendentals=0
        ),
        compiler_params=pltpu.CompilerParams(vmem_limit_bytes=32 * 2**20),
        name="decode_table",
    )(codes, scale.T)


def select_rows(wanted, table):
    peers, slots = wanted.shape
    rows, width = table.shape
    return pl.pallas_call(
        select_kernel,
        out_shape=jax.ShapeDtypeStruct((peers, slots, width), BF16),
        scratch_shapes=[pltpu.VMEM((slots, peers), jnp.int32)],
        cost_estimate=pl.CostEstimate(
            flops=2 * peers * slots * rows * width, bytes_accessed=3 * 2**20, transcendentals=0
        ),
        compiler_params=pltpu.CompilerParams(vmem_limit_bytes=32 * 2**20),
        name="select_rows",
    )(wanted, table)


def layer(live, summed, counts, rows, self_feat, grad_out, self_weight, neighbor_weight):
    targets, width = self_feat.shape
    cold = counts.shape[1]
    tile = 256
    by_tile = lambda w: pl.BlockSpec((tile, w), lambda i: (i, 0))
    return pl.pallas_call(
        layer_kernel,
        grid=(targets // tile,),
        in_specs=[
            pl.BlockSpec(memory_space=pltpu.SMEM),
            by_tile(width),
            by_tile(cold),
            whole(rows.shape),
            by_tile(width),
            by_tile(width),
            whole(self_weight.shape),
            whole(neighbor_weight.shape),
        ],
        out_specs=[by_tile(width), whole((2 * width, width))],
        out_shape=[
            jax.ShapeDtypeStruct((targets, width), BF16),
            jax.ShapeDtypeStruct((2 * width, width), BF16),
        ],
        scratch_shapes=[
            pltpu.VMEM((cold, width), BF16),
            pltpu.VMEM((cold, LANES), BF16),
            pltpu.VMEM((2 * width, width), F32),
        ],
        cost_estimate=pl.CostEstimate(
            flops=2 * targets * width * (cold + 4 * width),
            bytes_accessed=5 * 2**20,
            transcendentals=targets * width,
        ),
        compiler_params=pltpu.CompilerParams(vmem_limit_bytes=32 * 2**20),
        name="layer",
    )(live, summed, counts, rows, self_feat, grad_out, self_weight, neighbor_weight)


def exchange(parts, axes):
    return lax.all_to_all(parts, axes, split_axis=0, concat_axis=0, tiled=True)


def sum_everywhere(grads):
    rows, width = grads.shape
    plane = ("grp", "own")
    peers = lax.axis_size("grp") * lax.axis_size("own")
    depth = lax.axis_size("rep")
    parts = exchange(grads.reshape(peers, rows // peers, width), plane)
    share = jnp.sum(parts.astype(F32), axis=0)
    shares = exchange(jnp.broadcast_to(share[None], (depth,) + share.shape), "rep")
    share = jnp.sum(shares, axis=0).astype(BF16)
    parts = exchange(jnp.broadcast_to(share[None], (peers,) + share.shape), plane)
    return parts.reshape(rows, width).astype(F32)


def body(
    self_feat,
    neighbor,
    grad_out,
    fetch_rows,
    fetch_count,
    table_codes,
    table_scale,
    hot_table,
    self_weight,
    neighbor_weight,
):
    owners, slots = fetch_rows.shape
    width = self_feat.shape[1]
    wanted = exchange(fetch_rows, "own")
    table = decode_table(table_codes, table_scale)
    summed, counts = count_rows(neighbor, self_feat, hot_table, owners * slots)
    rows = exchange(select_rows(wanted, table), "own")
    hidden, grads = layer(
        fetch_count, summed, counts, rows, self_feat, grad_out, self_weight, neighbor_weight
    )
    total = sum_everywhere(grads)
    return hidden, total[:width], total[width:]


def solution(mesh):
    split = P(("grp", "own", "rep"), None)
    in_specs = (
        split,
        split,
        split,
        split,
        P(("grp", "own", "rep")),
        P("own", None),
        P("own", None),
        P(),
        P(),
        P(),
    )
    out_specs = (split, P(), P())
    return jax.shard_map(body, mesh=mesh, in_specs=in_specs, out_specs=out_specs, check_vma=False)
```

time: 710 us -> 108 us (0.15)
  waiting for transfers between devices: 468 us -> 0.83 us
  local copies, waits for them, and re-layouts: 179 us -> 8.08 us
  blocking collectives: 0 us -> 60.3 us
  Pallas kernels: 0 us -> 19.5 us
  other arithmetic: 15.7 us -> 0.12 us
  between operations: 14.2 us -> 0.71 us
  matrix products: 7.18 us -> 0 us
    psum x1 -> x0, waiting for transfers between devices: 465 us -> none  [body(): grad_self, grad_nbr = lax.psum((grad_self, grad_nbr), ('grp', 'own', 'rep'))]
    gather x6 -> x0, local copies, waits for them, and re-layouts: 157 us -> none  [the longest x2 85.3 us: body(): divisor = (1 + jnp.sum(pool_live[neighbor], axis=1)).astype(jnp.float32)]
    all_to_all x0 -> x3, blocking collectives: none -> 60.3 us  [exchange(): return lax.all_to_all(parts, axes, split_axis=0, concat_axis=0, tiled=True)]
    pallas_call x0 -> x4, Pallas kernels: none -> 19.5 us  [the longest x1 9.6 us: count_rows(): pl.pallas_call(count_kernel, grid=(targets // tile,), in_specs=[pl.BlockS...]
    convert_element_type x3 -> x0, local copies, waits for them, and re-layouts: 13.9 us -> none  [the longest x1 12.9 us: body(): jnp.sum(picked, axis=1, dtype=jnp.float32)]
    reduce_sum x2, other arithmetic: 10.1 us -> 0.09 us  [the longest x1 0.07 us: sum_everywhere(): share = jnp.sum(parts.astype(F32), axis=0)]
    dot_general x4 -> x0, matrix products: 7.18 us -> none  [the longest x1 2.66 us: body(): jnp.dot(mean_feat, neighbor_weight, preferred_element_type=jnp.float32)]
    all_to_all x3 -> x2, starting transfers between devices: 23.5 us -> 17.8 us  [exchange(): return lax.all_to_all(parts, axes, split_axis=0, concat_axis=0, tiled=True)]
  transfers between devices with their start and end apart: 4 -> 2, of which waited for: 2 -> 1; matrix products, arithmetic and copies ran while one was open for 14% -> 0% of each run, Pallas kernels for 0% -> 10%
where the time goes in v1:
time: 108 us; the launch traced here: 107 us
  blocking collectives  60.3 us (56%)
  Pallas kernels  19.5 us (18%)
  starting transfers between devices  17.8 us (16%)
  local copies, waits for them, and re-layouts  8.08 us (7%)
    all_to_all x3, blocking collectives, exchange(): return lax.all_to_all(parts, axes, split_axis=0, concat_axis=0, tiled=True)  60.3 us
    all_to_all x2, starting transfers between devices, exchange(): return lax.all_to_all(parts, axes, split_axis=0, concat_axis=0, tiled=True)  17.8 us
    pallas_call x1, Pallas kernels, count_rows(): pl.pallas_call(count_kernel, grid=(targets // tile,), in_specs=[pl.BlockS...  9.6 us
    unnamed x18, local copies, waits for them, and re-layouts  7.23 us
    pallas_call x1, Pallas kernels, layer(): pl.pallas_call(layer_kernel, grid=(targets // tile,), in_specs=[pl.BlockS...  4.93 us
    pallas_call x1, Pallas kernels, select_rows(): pl.pallas_call(select_kernel, out_shape=jax.ShapeDtypeStruct((peers, slot...  3.63 us
  transfers between devices with their start and end apart: 2, of which 1 were waited for; matrix products, arithmetic and copies ran while one was open for 0% of the time, Pallas kernels for 10%

profile of v1, /device:TPU:1, one launch (start us, length us, event | category | flops | bytes accessed | tf_op | source)
XLA Modules:
  0.0 107.4 jit_solution(13027031199158605263)
XLA Ops:
  0.6 13.7 %all-to-all-start = ((s32[8,1,96]{2,1,0:T(1,128)}), s32[8,1,96]{2,1,0:T(1,128)S(1)}, u32[]{:S(2)}, u32[]{:S(2)}) async-start(s32[8,1,96]{2,1,0:T(1,128)} %bitcast.13), calls=%async_computation | async-start | bytes 8192 | tf_op jit(solution)/shard_map/all_to_all | solution.py:236
  14.4 0.0 copy-start
  14.4 1.6 %copy-done = bf16[4096,256]{1,0:T(8,128)(2,1)S(1)} copy-done((bf16[4096,256]{1,0:T(8,128)(2,1)S(1)}, bf16[4096,256]{1,0:T(8,128)(2,1)}, u32[]{:S(2)}) %copy-start) | copy-done | bytes 2097176
  16.0 0.0 copy-start.5
  16.0 0.7 copy-done.5
  16.7 1.4 %decode_table.1.table_ref = bf16[4096,256]{1,0:T(8,128)(2,1)S(1)} custom-call(bf16[4096,256]{1,0:T(8,128)(2,1)S(1)} %copy-done, bf16[2,4096]{1,0:T(2,128)(2,1)S(1)} %bitcast.10), custom_call_target="tpu_custom_call" | custom-call | flops 2097152 | bytes 4194304 | tf_op jit(solution)/shard_map/decode_table/pallas_call | solution.py:165
  18.1 0.8 all-to-all-done
  18.9 0.0 copy-start.1
  18.9 3.6 %select_rows.1 = bf16[8,96,256]{2,1,0:T(8,128)(2,1)} custom-call(s32[8,96]{1,0:T(8,128)S(1)} %bitcast.11, bf16[4096,256]{1,0:T(8,128)(2,1)S(1)} %decode_table.1.table_ref), custom_call_target="tpu_custom_call" | custom-call | flops 1610612736 | bytes 3145728 | tf_op jit(solution)/shard_map/select_rows/pallas_call | solution.py:185
  22.5 4.0 %all-to-all-start.1 = ((bf16[8,96,256]{2,1,0:T(8,128)(2,1)}), bf16[8,96,256]{2,1,0:T(8,128)(2,1)S(1)}, u32[]{:S(2)}, u32[]{:S(2)}) async-start(bf16[8,96,256]{2,1,0:T(8,128)(2,1)} %select_rows.1), calls=%async_computation.1 | async-start | bytes 786432 | tf_op jit(solution)/shard_map/all_to_all | solution.py:236
  26.6 0.0 copy-start.6
  26.6 0.0 copy-done.1
  26.6 0.0 copy-start.7
  26.6 1.2 %copy-done.7 = bf16[2048,256]{1,0:T(8,128)(2,1)S(1)} copy-done((bf16[2048,256]{1,0:T(8,128)(2,1)S(1)}, bf16[2048,256]{1,0:T(8,128)(2,1)}, u32[]{:S(2)}) %copy-start.7) | copy-done | bytes 1048600
  27.8 0.0 copy-start.8
  27.8 0.8 copy-done.8
  28.6 9.6 %count_rows.1 = (f32[1024,256]{1,0:T(8,128)S(1)}, bf16[1024,768]{1,0:T(8,128)(2,1)S(1)}) custom-call(s32[15,1024]{1,0:T(8,128)S(1)} %bitcast.12, bf16[1024,256]{1,0:T(8,128)(2,1)S(1)} %copy-done.1, bf16[2048,256]{1,0:T(8,128)(2,1)S(1)} %copy-done.7), custom_call_target="tpu_custom_call" | custom-call | flops 1073741824 | bytes 16777216 | tf_op jit(solution)/shard_map/count_rows/pallas_call | solution.py:136
  38.3 0.0 all-to-all-done.1.rows_ref
  38.3 0.0 copy-done.6
  38.3 0.0 copy-start.2
  38.3 1.0 copy-done.2
  39.3 0.0 copy-start.3
  39.3 0.9 copy-done.3
  40.2 0.0 copy-start.4
  40.2 0.9 copy-done.4
  41.1 4.9 %layer.1 = (bf16[1024,256]{1,0:T(8,128)(2,1)}, bf16[512,256]{1,0:T(8,128)(2,1)S(1)}) custom-call(s32[8]{0:T(128)S(1)} %copy-done.6, f32[1024,256]{1,0:T(8,128)S(1)} %get-tuple-element.7.sum_ref, bf16[1024,768]{1,0:T(8,128)(2,1)S(1)} %get-tuple-element.8.counts_ref, bf16[8,96,256]{2,1,0:T(8,128)(2,1)S(1)} %all-to-all-done.1.rows_ref, ...), custom_call_target="tpu_custom_call" | custom-call | flops 939524096 | bytes 5242880 | tf_op jit(solution)/shard_map/layer/pallas_call | solution.py:202
  46.1 18.3 %all_to_all.31 = bf16[64,8,256]{2,1,0:T(8,128)(2,1)S(1)} all-to-all(bf16[64,8,256]{2,1,0:T(8,128)(2,1)S(1)} %bitcast.9), channel_id=1, replica_groups=mesh['grp'=8,'own'=8,'rep'=12] {'grp','own'}, dimensions={0} | all-to-all | bytes 524288 | tf_op jit(solution)/shard_map/all_to_all | solution.py:236
  64.4 0.1 convert_reduce_fusion
  64.5 22.4 %all_to_all.32 = f32[12,8,256]{2,1,0:T(8,128)S(1)} all-to-all(f32[12,8,256]{2,1,0:T(8,128)S(1)} %broadcast_in_dim.4), channel_id=1, replica_groups=mesh['grp'=8,'own'=8,'rep'=12] {'rep'}, dimensions={0} | all-to-all | bytes 196608 | tf_op jit(solution)/shard_map/all_to_all | solution.py:236
  86.9 19.6 %all_to_all.33 = bf16[64,8,256]{2,1,0:T(8,128)(2,1)S(1)} all-to-all(bf16[64,8,256]{2,1,0:T(8,128)(2,1)S(1)} %broadcast_in_dim.5), channel_id=1, replica_groups=mesh['grp'=8,'own'=8,'rep'=12] {'grp','own'}, dimensions={0} | all-to-all | bytes 524288 | tf_op jit(solution)/shard_map/all_to_all | solution.py:236
  106.6 0.8 slice_bitcast_fusion
  (4 shorter events, 0.1 us)
Async XLA Ops:
  0.6 18.3 %all-to-all-start = ((s32[8,1,96]{2,1,0:T(1,128)}), s32[8,1,96]{2,1,0:T(1,128)S(1)}, u32[]{:S(2)}, u32[]{:S(2)}) async-start(s32[8,1,96]{2,1,0:T(1,128)} %bitcast.13), calls=%async_computation | async-start | bytes 8192 | tf_op jit(solution)/shard_map/all_to_all | solution.py:236
  14.4 1.6 %copy-start = (bf16[4096,256]{1,0:T(8,128)(2,1)S(1)}, bf16[4096,256]{1,0:T(8,128)(2,1)}, u32[]{:S(2)}) copy-start(bf16[4096,256]{1,0:T(8,128)(2,1)} %code_ref.1) | copy-start | bytes 6291460
  16.0 0.7 copy-start.5
  18.9 7.7 %copy-start.1 = (bf16[1024,256]{1,0:T(8,128)(2,1)S(1)}, bf16[1024,256]{1,0:T(8,128)(2,1)}, u32[]{:S(2)}) copy-start(bf16[1024,256]{1,0:T(8,128)(2,1)} %self_ref.3) | copy-start | bytes 1572868
  22.5 15.7 %all-to-all-start.1 = ((bf16[8,96,256]{2,1,0:T(8,128)(2,1)}), bf16[8,96,256]{2,1,0:T(8,128)(2,1)S(1)}, u32[]{:S(2)}, u32[]{:S(2)}) async-start(bf16[8,96,256]{2,1,0:T(8,128)(2,1)} %select_rows.1), calls=%async_computation.1 | async-start | bytes 786432 | tf_op jit(solution)/shard_map/all_to_all | solution.py:236
  26.6 11.7 %copy-start.6 = (s32[8]{0:T(128)S(1)}, s32[8]{0:T(128)}, u32[]{:S(2)}) copy-start(s32[8]{0:T(128)} %live_ref.1) | copy-start | bytes 100
  26.6 1.2 %copy-start.7 = (bf16[2048,256]{1,0:T(8,128)(2,1)S(1)}, bf16[2048,256]{1,0:T(8,128)(2,1)}, u32[]{:S(2)}) copy-start(bf16[2048,256]{1,0:T(8,128)(2,1)} %hot_ref.1) | copy-start | bytes 3145732
  27.8 0.8 copy-start.8
  38.3 1.0 copy-start.2
  39.3 0.9 copy-start.3
  40.2 0.9 copy-start.4

commit v2 on v1

v2 whole, which is shorter than its diff:
```python
import jax
import jax.numpy as jnp
from jax import lax
from jax.experimental import pallas as pl
from jax.experimental.pallas import tpu as pltpu
from jax.sharding import PartitionSpec as P

F32 = jnp.float32
BF16 = jnp.bfloat16
LANES = 128
STEP = 16
PEERS = 4
PARTS = 4
VMEM = 32 * 2**20


def counter(words, i):
    if i:
        words = lax.shift_right_logical(words, 4 * i)
    if i < 7:
        words = jnp.bitwise_and(words, 15)
    return words.astype(F32).astype(BF16)


def count_kernel(
    nbr_hbm,
    hot_hbm,
    self_hbm,
    grad_hbm,
    self_w_hbm,
    nbr_w_hbm,
    sum_ref,
    cold_ref,
    held_ref,
    nbr_ref,
    hot_ref,
    keys_ref,
    counts_ref,
    sems,
):
    moves = [(nbr_hbm, nbr_ref), (hot_hbm, hot_ref)]
    start = 0
    for array in (self_hbm, grad_hbm, self_w_hbm, nbr_w_hbm):
        moves.append((array, held_ref.at[start : start + array.shape[0]]))
        start += array.shape[0]
    copies = [pltpu.make_async_copy(*move, sems.at[i]) for i, move in enumerate(moves)]
    for copy in copies:
        copy.start()
    neighbors, targets = nbr_ref.shape
    hot_blocks = hot_ref.shape[0] // LANES
    groups = hot_blocks // 8 + 1
    steps = LANES // STEP

    copies[0].wait()
    rows = nbr_ref[...]
    keys_ref[0, :neighbors, :] = jnp.bitwise_and(rows, LANES - 1)
    bit = jnp.left_shift(jnp.int32(1), jnp.bitwise_and(jnp.right_shift(rows, 5), 28))
    group = jnp.right_shift(rows, 10)
    for g in range(groups):
        keys_ref[1 + g, :neighbors, :] = jnp.where(group == g, bit, 0)

    def step(i, carry):
        cut = pl.ds(pl.multiple_of((i // steps) * LANES, LANES), LANES)
        base = pl.multiple_of((i % steps) * STEP, STEP)
        place = lax.broadcasted_iota(jnp.int32, (STEP, LANES), 0) + base
        words = [jnp.zeros((STEP, LANES), jnp.int32) for _ in range(groups)]
        for k in range(neighbors):
            spread = lambda r: jnp.broadcast_to(keys_ref[r, k : k + 1, cut], (STEP, LANES))
            here = spread(0) == place
            for g in range(groups):
                words[g] = words[g] + jnp.where(here, spread(1 + g), 0)
        for b in range(hot_blocks):
            counts_ref[pl.ds(b * LANES + base, STEP), cut] = counter(words[b // 8], b % 8)
        cold_ref[pl.ds(base, STEP), cut] = words[groups - 1]
        return carry

    lax.fori_loop(0, (targets // LANES) * steps, step, 0, unroll=2)
    for copy in copies[1:]:
        copy.wait()
    sum_ref[...] = held_ref[:targets, :].astype(F32).T + lax.dot_general(
        hot_ref[...], counts_ref[...], (((0,), (0,)), ((), ())), preferred_element_type=F32
    )


def decode_kernel(code_hbm, scale_hbm, out_ref, code_ref, scale_ref, sems):
    rows, width = code_ref.shape
    blocks = scale_ref.shape[0]
    part = rows // PARTS
    scale_copy = pltpu.make_async_copy(scale_hbm, scale_ref, sems.at[PARTS])
    scale_copy.start()
    cuts = [slice(i * part, (i + 1) * part) for i in range(PARTS)]
    copies = [
        pltpu.make_async_copy(code_hbm.at[cut], code_ref.at[cut], sems.at[i])
        for i, cut in enumerate(cuts)
    ]
    for copy in copies:
        copy.start()
    which = lax.broadcasted_iota(jnp.int32, (blocks, width), 0)
    block = lax.broadcasted_iota(jnp.int32, (blocks, width), 1) // (width // blocks)
    ones = jnp.where(which == block, 1.0, 0.0).astype(BF16)
    scale_copy.wait()
    for cut, copy in zip(cuts, copies):
        scale = lax.dot_general(
            scale_ref[:, cut], ones, (((0,), (0,)), ((), ())), preferred_element_type=F32
        )
        copy.wait()
        out_ref[cut] = (code_ref[cut].astype(F32) * scale).astype(BF16)


def select_kernel(want_ref, table_ref, out_ref, cols_ref):
    peers, slots = want_ref.shape
    rows, width = table_ref.shape
    cols_ref[...] = want_ref[...].T
    lane = lax.broadcasted_iota(jnp.int32, (slots, rows), 1)
    for p in range(0, peers, PEERS):
        picks = [
            jnp.where(jnp.broadcast_to(cols_ref[:, q : q + 1], (slots, rows)) == lane, 1.0, 0.0)
            for q in range(p, p + PEERS)
        ]
        pick = jnp.concatenate(picks, axis=0).astype(BF16)
        found = jnp.dot(pick, table_ref[...], preferred_element_type=F32).astype(BF16)
        out_ref[p : p + PEERS] = found.reshape(PEERS, slots, width)


def layer_kernel(
    live_ref,
    sum_ref,
    words_ref,
    rows_ref,
    held_ref,
    hidden_hbm,
    grads_ref,
    cold_ref,
    hidden_ref,
    sem,
):
    owners, slots, width = rows_ref.shape
    targets = sum_ref.shape[1]
    rows = []
    for p in range(owners):
        slot = lax.broadcasted_iota(jnp.int32, (slots, width), 0)
        rows.append(jnp.where(slot < live_ref[p], rows_ref[p].astype(F32), 0.0))
    cold_ref[:width, :] = jnp.concatenate(rows, axis=0).T.astype(BF16)
    dead = [
        jnp.where(lax.broadcasted_iota(jnp.int32, (1, slots), 1) < live_ref[p], 0.0, 1.0)
        for p in range(owners)
    ]
    dead = jnp.broadcast_to(jnp.concatenate(dead, axis=1), (STEP, owners * slots))
    cold_ref[width:, :] = dead.astype(BF16)

    words = words_ref[...]
    blocks = owners * slots // LANES
    counts = jnp.concatenate([counter(words, b) for b in range(blocks)], axis=0)
    cold = jnp.dot(cold_ref[...], counts, preferred_element_type=F32)
    share = 1.0 / (16.0 - cold[width : width + 1, :])
    mean_t = ((sum_ref[...] + cold[:width, :]) * share).astype(BF16)
    mean = mean_t.T
    own = held_ref[:targets, :]
    weights = 2 * targets
    pre = jnp.dot(own, held_ref[weights : weights + width, :], preferred_element_type=F32) + jnp.dot(
        mean, held_ref[weights + width :, :], preferred_element_type=F32
    )
    sigma = 1.0 / (1.0 + jnp.exp(-pre))
    hidden_ref[...] = (pre * sigma).astype(BF16)
    out = pltpu.make_async_copy(hidden_ref, hidden_hbm, sem)
    out.start()
    slope = sigma * (1.0 + pre * (1.0 - sigma))
    delta = (held_ref[targets:weights, :].astype(F32) * slope).astype(BF16)
    across = (((0,), (0,)), ((), ()))
    grads_ref[:width, :] = lax.dot_general(
        own, delta, across, preferred_element_type=F32
    ).astype(BF16)
    grads_ref[width:, :] = jnp.dot(mean_t, delta, preferred_element_type=F32).astype(BF16)
    out.wait()


def outside(array):
    return pltpu.with_memory_space_constraint(array, pltpu.HBM)


def inside(array):
    return pltpu.with_memory_space_constraint(array, pltpu.VMEM)


def count_rows(neighbor, hot_table, self_feat, grad_out, self_weight, neighbor_weight):
    targets, width = self_feat.shape
    neighbors = neighbor.shape[1]
    hot = hot_table.shape[0]
    passed = (self_feat, grad_out, self_weight, neighbor_weight)
    arrays = (neighbor.T, hot_table) + passed
    return pl.pallas_call(
        count_kernel,
        in_specs=[pl.BlockSpec(memory_space=pltpu.HBM)] * len(arrays),
        out_shape=[
            jax.ShapeDtypeStruct((width, targets), F32),
            jax.ShapeDtypeStruct((LANES, targets), jnp.int32),
            jax.ShapeDtypeStruct((sum(array.shape[0] for array in passed), width), BF16),
        ],
        scratch_shapes=[
            pltpu.VMEM((neighbors, targets), jnp.int32),
            pltpu.VMEM((hot, width), BF16),
            pltpu.VMEM((4, 16, targets), jnp.int32),
            pltpu.VMEM((hot, targets), BF16),
            pltpu.SemaphoreType.DMA((len(arrays),)),
        ],
        cost_estimate=pl.CostEstimate(
            flops=2 * targets * hot * width, bytes_accessed=16 * 2**20, transcendentals=0
        ),
        compiler_params=pltpu.CompilerParams(vmem_limit_bytes=VMEM),
        name="count_rows",
    )(*map(outside, arrays))


def decode_table(codes, scale):
    rows, width = codes.shape
    blocks = scale.shape[1]
    return pl.pallas_call(
        decode_kernel,
        in_specs=[pl.BlockSpec(memory_space=pltpu.HBM)] * 2,
        out_shape=jax.ShapeDtypeStruct((rows, width), BF16),
        scratch_shapes=[
            pltpu.VMEM((rows, width), BF16),
            pltpu.VMEM((blocks, rows), BF16),
            pltpu.SemaphoreType.DMA((PARTS + 1,)),
        ],
        cost_estimate=pl.CostEstimate(
            flops=2 * rows * width, bytes_accessed=4 * 2**20, transcendentals=0
        ),
        compiler_params=pltpu.CompilerParams(vmem_limit_bytes=VMEM),
        name="decode_table",
    )(outside(codes), outside(scale.T))


def select_rows(wanted, table):
    peers, slots = wanted.shape
    rows, width = table.shape
    return pl.pallas_call(
        select_kernel,
        out_shape=jax.ShapeDtypeStruct((peers, slots, width), BF16),
        scratch_shapes=[pltpu.VMEM((slots, peers), jnp.int32)],
        cost_estimate=pl.CostEstimate(
            flops=2 * peers * slots * rows * width, bytes_accessed=3 * 2**20, transcendentals=0
        ),
        compiler_params=pltpu.CompilerParams(vmem_limit_bytes=VMEM),
        name="select_rows",
    )(wanted, table)


def layer(live, *arrays):
    summed, _, rows, _ = arrays
    width, targets = summed.shape
    cold = rows.shape[0] * rows.shape[1]
    near = pl.BlockSpec(memory_space=pltpu.VMEM)
    return pl.pallas_call(
        layer_kernel,
        in_specs=[pl.BlockSpec(memory_space=pltpu.SMEM)] + [near] * len(arrays),
        out_specs=[pl.BlockSpec(memory_space=pltpu.HBM), near],
        out_shape=[
            jax.ShapeDtypeStruct((targets, width), BF16),
            jax.ShapeDtypeStruct((2 * width, width), BF16),
        ],
        scratch_shapes=[
            pltpu.VMEM((width + STEP, cold), BF16),
            pltpu.VMEM((targets, width), BF16),
            pltpu.SemaphoreType.DMA,
        ],
        cost_estimate=pl.CostEstimate(
            flops=2 * targets * width * (cold + 4 * width),
            bytes_accessed=5 * 2**20,
            transcendentals=targets * width,
        ),
        compiler_params=pltpu.CompilerParams(vmem_limit_bytes=VMEM),
        name="layer",
    )(live, *map(inside, arrays))


def exchange(parts, axes):
    return lax.all_to_all(parts, axes, split_axis=0, concat_axis=0, tiled=True)


def sum_everywhere(grads):
    rows, width = grads.shape
    plane = ("grp", "own")
    peers = lax.axis_size("grp") * lax.axis_size("own")
    depth = lax.axis_size("rep")
    parts = exchange(grads.reshape(peers, rows // peers, width), plane)
    share = jnp.sum(parts.astype(F32), axis=0)
    shares = exchange(jnp.broadcast_to(share[None], (depth,) + share.shape), "rep")
    share = jnp.sum(shares, axis=0).astype(BF16)
    parts = exchange(jnp.broadcast_to(share[None], (peers,) + share.shape), plane)
    return parts.reshape(rows, width).astype(F32)


def body(
    self_feat,
    neighbor,
    grad_out,
    fetch_rows,
    fetch_count,
    table_codes,
    table_scale,
    hot_table,
    self_weight,
    neighbor_weight,
):
    width = self_feat.shape[1]
    wanted = exchange(fetch_rows, "own")
    table = decode_table(table_codes, table_scale)
    summed, words, held = count_rows(
        neighbor, hot_table, self_feat, grad_out, self_weight, neighbor_weight
    )
    rows = exchange(select_rows(wanted, table), "own")
    hidden, grads = layer(fetch_count, summed, words, rows, held)
    total = sum_everywhere(grads)
    return hidden, total[:width], total[width:]


def solution(mesh):
    split = P(("grp", "own", "rep"), None)
    in_specs = (
        split,
        split,
        split,
        split,
        P(("grp", "own", "rep")),
        P("own", None),
        P("own", None),
        P(),
        P(),
        P(),
    )
    out_specs = (split, P(), P())
    return jax.shard_map(body, mesh=mesh, in_specs=in_specs, out_specs=out_specs, check_vma=False)
```

time: 108 us -> 96.9 us (0.90)
  local copies, waits for them, and re-layouts: 8.08 us -> 0.86 us
  Pallas kernels: 19.5 us -> 15.2 us
  waiting for transfers between devices: 0.83 us -> 3.08 us
  blocking collectives: 60.3 us -> 58.8 us
    unnamed x18 -> x2, local copies, waits for them, and re-layouts: 7.23 us -> 0.01 us
    pallas_call x3, Pallas kernels: 15.9 us -> 12.5 us  [the longest x1 6.32 us: count_rows(): pl.pallas_call(count_kernel, in_specs=[pl.BlockSpec(memory_space=pltpu.HB...]
    all_to_all x2, waiting for transfers between devices: 0.83 us -> 3.08 us  [exchange(): return lax.all_to_all(parts, axes, split_axis=0, concat_axis=0, tiled=True)]
    all_to_all x3, blocking collectives: 60.3 us -> 58.8 us  [exchange(): return lax.all_to_all(parts, axes, split_axis=0, concat_axis=0, tiled=True)]
  transfers between devices with their start and end apart: 2 -> 2, of which waited for: 1 -> 2; matrix products, arithmetic and copies ran while one was open for 0% -> 0% of each run, Pallas kernels for 10% -> 10%
where the time goes in v2:
time: 96.9 us; the launch traced here: 96.5 us
  blocking collectives  58.8 us (61%)
  starting transfers between devices  17.8 us (18%)
  Pallas kernels  15.2 us (16%)
  waiting for transfers between devices  3.08 us (3%)
    all_to_all x3, blocking collectives, exchange(): return lax.all_to_all(parts, axes, split_axis=0, concat_axis=0, tiled=True)  58.8 us
    all_to_all x2, starting transfers between devices, exchange(): return lax.all_to_all(parts, axes, split_axis=0, concat_axis=0, tiled=True)  17.8 us
    pallas_call x1, Pallas kernels, count_rows(): pl.pallas_call(count_kernel, in_specs=[pl.BlockSpec(memory_space=pltpu.HB...  6.32 us
    pallas_call x1, Pallas kernels, decode_table(): pl.pallas_call(decode_kernel, in_specs=[pl.BlockSpec(memory_space=pltpu.H...  3.2 us
    all_to_all x2, waiting for transfers between devices, exchange(): return lax.all_to_all(parts, axes, split_axis=0, concat_axis=0, tiled=True)  3.08 us
    pallas_call x1, Pallas kernels, layer(): pl.pallas_call(layer_kernel, in_specs=[pl.BlockSpec(memory_space=pltpu.SM...  2.96 us
    pallas_call x1, Pallas kernels, select_rows(): pl.pallas_call(select_kernel, out_shape=jax.ShapeDtypeStruct((peers, slot...  2.71 us
  transfers between devices with their start and end apart: 2, of which 2 were waited for; matrix products, arithmetic and copies ran while one was open for 0% of the time, Pallas kernels for 10%

profile of v2, /device:TPU:1, one launch (start us, length us, event | category | flops | bytes accessed | tf_op | source)
XLA Modules:
  0.0 96.5 jit_solution(433230994734526197)
XLA Ops:
  0.6 13.7 %all-to-all-start = ((s32[8,1,96]{2,1,0:T(1,128)}), s32[8,1,96]{2,1,0:T(1,128)S(1)}, u32[]{:S(2)}, u32[]{:S(2)}) async-start(s32[8,1,96]{2,1,0:T(1,128)} %bitcast.12), calls=%async_computation | async-start | bytes 8192 | tf_op jit(solution)/shard_map/all_to_all | solution.py:278
  14.4 3.2 %decode_table.1.table_ref = bf16[4096,256]{1,0:T(8,128)(2,1)S(1)} custom-call(bf16[4096,256]{1,0:T(8,128)(2,1)} %code_hbm.1, bf16[2,4096]{1,0:T(2,128)(2,1)} %bitcast.11), custom_call_target="tpu_custom_call" | custom-call | flops 2097152 | bytes 4194304 | tf_op jit(solution)/shard_map/decode_table/pallas_call | solution.py:217
  17.6 1.3 %all-to-all-done = s32[8,1,96]{2,1,0:T(1,128)S(1)} async-done(((s32[8,1,96]{2,1,0:T(1,128)}), s32[8,1,96]{2,1,0:T(1,128)S(1)}, u32[]{:S(2)}, u32[]{:S(2)}) %all-to-all-start) | async-done | bytes 3104 | tf_op jit(solution)/shard_map/all_to_all | solution.py:278
  18.9 2.7 %select_rows.1 = bf16[8,96,256]{2,1,0:T(8,128)(2,1)} custom-call(s32[8,96]{1,0:T(8,128)S(1)} %bitcast.10, bf16[4096,256]{1,0:T(8,128)(2,1)S(1)} %decode_table.1.table_ref), custom_call_target="tpu_custom_call" | custom-call | flops 1610612736 | bytes 3145728 | tf_op jit(solution)/shard_map/select_rows/pallas_call | solution.py:237
  21.6 4.1 %all-to-all-start.1 = ((bf16[8,96,256]{2,1,0:T(8,128)(2,1)}), bf16[8,96,256]{2,1,0:T(8,128)(2,1)S(1)}, u32[]{:S(2)}, u32[]{:S(2)}) async-start(bf16[8,96,256]{2,1,0:T(8,128)(2,1)} %select_rows.1), calls=%async_computation.1 | async-start | bytes 786432 | tf_op jit(solution)/shard_map/all_to_all | solution.py:278
  25.6 0.0 copy-start
  25.7 6.3 %count_rows.1 = (f32[256,1024]{1,0:T(8,128)S(1)}, s32[128,1024]{1,0:T(8,128)S(1)}, bf16[2560,256]{1,0:T(8,128)(2,1)S(1)}) custom-call(s32[15,1024]{1,0:T(8,128)} %bitcast.13, bf16[2048,256]{1,0:T(8,128)(2,1)} %hot_hbm.1, bf16[1024,256]{1,0:T(8,128)(2,1)} %self_hbm.1, bf16[1024,256]{1,0:T(8,128)(2,1)} %grad_hbm.1, bf16[256,256]{1,0:T(8,128)(2,1)} %self_w_hbm.1, ...), custom_call_target="tpu_custom_call" | custom-call | flops 1073741824 | bytes 16777216 | tf_op jit(solution)/shard_map/count_rows/pallas_call | solution.py:191
  32.0 1.8 %all-to-all-done.1.rows_ref = bf16[8,96,256]{2,1,0:T(8,128)(2,1)S(1)} async-done(((bf16[8,96,256]{2,1,0:T(8,128)(2,1)}), bf16[8,96,256]{2,1,0:T(8,128)(2,1)S(1)}, u32[]{:S(2)}, u32[]{:S(2)}) %all-to-all-start.1) | async-done | bytes 393248 | tf_op jit(solution)/shard_map/all_to_all | solution.py:278
  33.7 0.0 copy-done
  33.7 3.0 %layer.1 = (bf16[1024,256]{1,0:T(8,128)(2,1)}, bf16[512,256]{1,0:T(8,128)(2,1)S(1)}) custom-call(s32[8]{0:T(128)S(1)} %copy-done, f32[256,1024]{1,0:T(8,128)S(1)} %get-tuple-element.8.sum_ref, s32[128,1024]{1,0:T(8,128)S(1)} %get-tuple-element.9.words_ref, bf16[8,96,256]{2,1,0:T(8,128)(2,1)S(1)} %all-to-all-done.1.rows_ref, ...), custom_call_target="tpu_custom_call" | custom-call | flops 939524096 | bytes 5242880 | tf_op jit(solution)/shard_map/layer/pallas_call | solution.py:254
  36.7 17.4 %all_to_all.31 = bf16[64,8,256]{2,1,0:T(8,128)(2,1)S(1)} all-to-all(bf16[64,8,256]{2,1,0:T(8,128)(2,1)S(1)} %bitcast.9), channel_id=1, replica_groups=mesh['grp'=8,'own'=8,'rep'=12] {'grp','own'}, dimensions={0} | all-to-all | bytes 524288 | tf_op jit(solution)/shard_map/all_to_all | solution.py:278
  54.1 0.1 convert_reduce_fusion
  54.2 21.8 %all_to_all.32 = f32[12,8,256]{2,1,0:T(8,128)S(1)} all-to-all(f32[12,8,256]{2,1,0:T(8,128)S(1)} %broadcast_in_dim.4), channel_id=1, replica_groups=mesh['grp'=8,'own'=8,'rep'=12] {'rep'}, dimensions={0} | all-to-all | bytes 196608 | tf_op jit(solution)/shard_map/all_to_all | solution.py:278
  76.0 19.6 %all_to_all.33 = bf16[64,8,256]{2,1,0:T(8,128)(2,1)S(1)} all-to-all(bf16[64,8,256]{2,1,0:T(8,128)(2,1)S(1)} %broadcast_in_dim.5), channel_id=1, replica_groups=mesh['grp'=8,'own'=8,'rep'=12] {'grp','own'}, dimensions={0} | all-to-all | bytes 524288 | tf_op jit(solution)/shard_map/all_to_all | solution.py:278
  95.7 0.8 slice_bitcast_fusion
  (4 shorter events, 0.1 us)
Async XLA Ops:
  0.6 18.3 %all-to-all-start = ((s32[8,1,96]{2,1,0:T(1,128)}), s32[8,1,96]{2,1,0:T(1,128)S(1)}, u32[]{:S(2)}, u32[]{:S(2)}) async-start(s32[8,1,96]{2,1,0:T(1,128)} %bitcast.12), calls=%async_computation | async-start | bytes 8192 | tf_op jit(solution)/shard_map/all_to_all | solution.py:278
  21.6 12.2 %all-to-all-start.1 = ((bf16[8,96,256]{2,1,0:T(8,128)(2,1)}), bf16[8,96,256]{2,1,0:T(8,128)(2,1)S(1)}, u32[]{:S(2)}, u32[]{:S(2)}) async-start(bf16[8,96,256]{2,1,0:T(8,128)(2,1)} %select_rows.1), calls=%async_computation.1 | async-start | bytes 786432 | tf_op jit(solution)/shard_map/all_to_all | solution.py:278
  25.6 8.1 %copy-start = (s32[8]{0:T(128)S(1)}, s32[8]{0:T(128)}, u32[]{:S(2)}) copy-start(s32[8]{0:T(128)} %live_ref.1) | copy-start | bytes 100

commit v3 on v2

--- a/solution.py
+++ b/solution.py
@@ -8,7 +8,7 @@
 F32 = jnp.float32
 BF16 = jnp.bfloat16
 LANES = 128
-STEP = 16
+STEP = 32
 PEERS = 4
 PARTS = 4
 VMEM = 32 * 2**20
@@ -23,7 +23,7 @@
 
 
 def count_kernel(
-    nbr_hbm,
+    nbr_ref,
     hot_hbm,
     self_hbm,
     grad_hbm,
@@ -32,30 +32,30 @@
     sum_ref,
     cold_ref,
     held_ref,
-    nbr_ref,
+    grad_ref,
     hot_ref,
     keys_ref,
     counts_ref,
     sems,
 ):
-    moves = [(nbr_hbm, nbr_ref), (hot_hbm, hot_ref)]
+    moves = [(hot_hbm, hot_ref), (grad_hbm, grad_ref)]
     start = 0
-    for array in (self_hbm, grad_hbm, self_w_hbm, nbr_w_hbm):
+    for array in (self_hbm, self_w_hbm, nbr_w_hbm):
         moves.append((array, held_ref.at[start : start + array.shape[0]]))
         start += array.shape[0]
     copies = [pltpu.make_async_copy(*move, sems.at[i]) for i, move in enumerate(moves)]
     for copy in copies:
         copy.start()
-    neighbors, targets = nbr_ref.shape
+    targets = nbr_ref.shape[1]
     hot_blocks = hot_ref.shape[0] // LANES
     groups = hot_blocks // 8 + 1
     steps = LANES // STEP
 
-    copies[0].wait()
-    rows = nbr_ref[...]
-    keys_ref[0, :neighbors, :] = jnp.bitwise_and(rows, LANES - 1)
-    bit = jnp.left_shift(jnp.int32(1), jnp.bitwise_and(jnp.right_shift(rows, 5), 28))
-    group = jnp.right_shift(rows, 10)
+    neighbors = nbr_ref.shape[0]
+    picks = nbr_ref[...]
+    keys_ref[0, :neighbors, :] = jnp.bitwise_and(picks, LANES - 1)
+    bit = jnp.left_shift(jnp.int32(1), jnp.bitwise_and(jnp.right_shift(picks, 5), 28))
+    group = jnp.right_shift(picks, 10)
     for g in range(groups):
         keys_ref[1 + g, :neighbors, :] = jnp.where(group == g, bit, 0)
 
@@ -74,20 +74,24 @@
         cold_ref[pl.ds(base, STEP), cut] = words[groups - 1]
         return carry
 
-    lax.fori_loop(0, (targets // LANES) * steps, step, 0, unroll=2)
-    for copy in copies[1:]:
+    lax.fori_loop(0, (targets // LANES) * steps, step, 0)
+    for copy in copies:
         copy.wait()
     sum_ref[...] = held_ref[:targets, :].astype(F32).T + lax.dot_general(
         hot_ref[...], counts_ref[...], (((0,), (0,)), ((), ())), preferred_element_type=F32
     )
 
 
-def decode_kernel(code_hbm, scale_hbm, out_ref, code_ref, scale_ref, sems):
+def prepare_kernel(
+    nbr_hbm, code_hbm, scale_hbm, nbr_ref, out_ref, code_ref, scale_ref, sems
+):
     rows, width = code_ref.shape
     blocks = scale_ref.shape[0]
     part = rows // PARTS
     scale_copy = pltpu.make_async_copy(scale_hbm, scale_ref, sems.at[PARTS])
     scale_copy.start()
+    nbr_copy = pltpu.make_async_copy(nbr_hbm, nbr_ref, sems.at[PARTS + 1])
+    nbr_copy.start()
     cuts = [slice(i * part, (i + 1) * part) for i in range(PARTS)]
     copies = [
         pltpu.make_async_copy(code_hbm.at[cut], code_ref.at[cut], sems.at[i])
@@ -99,12 +103,13 @@
     block = lax.broadcasted_iota(jnp.int32, (blocks, width), 1) // (width // blocks)
     ones = jnp.where(which == block, 1.0, 0.0).astype(BF16)
     scale_copy.wait()
+    scale = lax.dot_general(
+        scale_ref[...], ones, (((0,), (0,)), ((), ())), preferred_element_type=F32
+    )
     for cut, copy in zip(cuts, copies):
-        scale = lax.dot_general(
-            scale_ref[:, cut], ones, (((0,), (0,)), ((), ())), preferred_element_type=F32
-        )
         copy.wait()
-        out_ref[cut] = (code_ref[cut].astype(F32) * scale).astype(BF16)
+        out_ref[cut] = (code_ref[cut].astype(F32) * scale[cut]).astype(BF16)
+    nbr_copy.wait()
 
 
 def select_kernel(want_ref, table_ref, out_ref, cols_ref):
@@ -128,6 +133,7 @@
     words_ref,
     rows_ref,
     held_ref,
+    grad_ref,
     hidden_hbm,
     grads_ref,
     cold_ref,
@@ -156,16 +162,15 @@
     mean_t = ((sum_ref[...] + cold[:width, :]) * share).astype(BF16)
     mean = mean_t.T
     own = held_ref[:targets, :]
-    weights = 2 * targets
-    pre = jnp.dot(own, held_ref[weights : weights + width, :], preferred_element_type=F32) + jnp.dot(
-        mean, held_ref[weights + width :, :], preferred_element_type=F32
+    pre = jnp.dot(own, held_ref[targets : targets + width, :], preferred_element_type=F32) + jnp.dot(
+        mean, held_ref[targets + width :, :], preferred_element_type=F32
     )
     sigma = 1.0 / (1.0 + jnp.exp(-pre))
     hidden_ref[...] = (pre * sigma).astype(BF16)
     out = pltpu.make_async_copy(hidden_ref, hidden_hbm, sem)
     out.start()
     slope = sigma * (1.0 + pre * (1.0 - sigma))
-    delta = (held_ref[targets:weights, :].astype(F32) * slope).astype(BF16)
+    delta = (grad_ref[...].astype(F32) * slope).astype(BF16)
     across = (((0,), (0,)), ((), ()))
     grads_ref[:width, :] = lax.dot_general(
         own, delta, across, preferred_element_type=F32
@@ -182,22 +187,22 @@
     return pltpu.with_memory_space_constraint(array, pltpu.VMEM)
 
 
-def count_rows(neighbor, hot_table, self_feat, grad_out, self_weight, neighbor_weight):
+def count_rows(picks, hot_table, self_feat, grad_out, self_weight, neighbor_weight):
     targets, width = self_feat.shape
-    neighbors = neighbor.shape[1]
     hot = hot_table.shape[0]
-    passed = (self_feat, grad_out, self_weight, neighbor_weight)
-    arrays = (neighbor.T, hot_table) + passed
+    arrays = (hot_table, self_feat, grad_out, self_weight, neighbor_weight)
+    held = targets + self_weight.shape[0] + neighbor_weight.shape[0]
     return pl.pallas_call(
         count_kernel,
-        in_specs=[pl.BlockSpec(memory_space=pltpu.HBM)] * len(arrays),
+        in_specs=[pl.BlockSpec(memory_space=pltpu.VMEM)]
+        + [pl.BlockSpec(memory_space=pltpu.HBM)] * len(arrays),
         out_shape=[
             jax.ShapeDtypeStruct((width, targets), F32),
             jax.ShapeDtypeStruct((LANES, targets), jnp.int32),
-            jax.ShapeDtypeStruct((sum(array.shape[0] for array in passed), width), BF16),
+            jax.ShapeDtypeStruct((held, width), BF16),
+            jax.ShapeDtypeStruct((targets, width), BF16),
         ],
         scratch_shapes=[
-            pltpu.VMEM((neighbors, targets), jnp.int32),
             pltpu.VMEM((hot, width), BF16),
             pltpu.VMEM((4, 16, targets), jnp.int32),
             pltpu.VMEM((hot, targets), BF16),
@@ -208,27 +213,31 @@
         ),
         compiler_params=pltpu.CompilerParams(vmem_limit_bytes=VMEM),
         name="count_rows",
-    )(*map(outside, arrays))
-
-
-def decode_table(codes, scale):
+    )(picks, *map(outside, arrays))
+
+
+def prepare(neighbor, codes, scale):
     rows, width = codes.shape
     blocks = scale.shape[1]
+    targets, neighbors = neighbor.shape
     return pl.pallas_call(
-        decode_kernel,
-        in_specs=[pl.BlockSpec(memory_space=pltpu.HBM)] * 2,
-        out_shape=jax.ShapeDtypeStruct((rows, width), BF16),
+        prepare_kernel,
+        in_specs=[pl.BlockSpec(memory_space=pltpu.HBM)] * 3,
+        out_shape=[
+            jax.ShapeDtypeStruct((neighbors, targets), jnp.int32),
+            jax.ShapeDtypeStruct((rows, width), BF16),
+        ],
         scratch_shapes=[
             pltpu.VMEM((rows, width), BF16),
             pltpu.VMEM((blocks, rows), BF16),
-            pltpu.SemaphoreType.DMA((PARTS + 1,)),
+            pltpu.SemaphoreType.DMA((PARTS + 2,)),
         ],
         cost_estimate=pl.CostEstimate(
             flops=2 * rows * width, bytes_accessed=4 * 2**20, transcendentals=0
         ),
         compiler_params=pltpu.CompilerParams(vmem_limit_bytes=VMEM),
-        name="decode_table",
-    )(outside(codes), outside(scale.T))
+        name="prepare",
+    )(outside(neighbor.T), outside(codes), outside(scale.T))
 
 
 def select_rows(wanted, table):
@@ -246,15 +255,15 @@
     )(wanted, table)
 
 
-def layer(live, *arrays):
-    summed, _, rows, _ = arrays
+def layer(live, summed, words, rows, held, grad_out):
     width, targets = summed.shape
     cold = rows.shape[0] * rows.shape[1]
     near = pl.BlockSpec(memory_space=pltpu.VMEM)
+    far = pl.BlockSpec(memory_space=pltpu.HBM)
     return pl.pallas_call(
         layer_kernel,
-        in_specs=[pl.BlockSpec(memory_space=pltpu.SMEM)] + [near] * len(arrays),
-        out_specs=[pl.BlockSpec(memory_space=pltpu.HBM), near],
+        in_specs=[pl.BlockSpec(memory_space=pltpu.SMEM)] + [near] * 5,
+        out_specs=[far, near],
         out_shape=[
             jax.ShapeDtypeStruct((targets, width), BF16),
             jax.ShapeDtypeStruct((2 * width, width), BF16),
@@ -271,7 +280,7 @@
         ),
         compiler_params=pltpu.CompilerParams(vmem_limit_bytes=VMEM),
         name="layer",
-    )(live, *map(inside, arrays))
+    )(live, *map(inside, (summed, words, rows, held, grad_out)))
 
 
 def exchange(parts, axes):
@@ -305,12 +314,12 @@
 ):
     width = self_feat.shape[1]
     wanted = exchange(fetch_rows, "own")
-    table = decode_table(table_codes, table_scale)
-    summed, words, held = count_rows(
-        neighbor, hot_table, self_feat, grad_out, self_weight, neighbor_weight
+    picks, table = prepare(neighbor, table_codes, table_scale)
+    summed, words, held, grad_out = count_rows(
+        picks, hot_table, self_feat, grad_out, self_weight, neighbor_weight
     )
     rows = exchange(select_rows(wanted, table), "own")
-    hidden, grads = layer(fetch_count, summed, words, rows, held)
+    hidden, grads = layer(fetch_count, summed, words, rows, held, grad_out)
     total = sum_everywhere(grads)
     return hidden, total[:width], total[width:]
 

time: 96.9 us -> 96.9 us (level)
  Pallas kernels: 15.2 us -> 12.8 us
  waiting for transfers between devices: 3.08 us -> 5.47 us
    pallas_call x2, Pallas kernels: 9.52 us -> 7.13 us  [the longest x1 5.25 us: count_rows(): pl.pallas_call(count_kernel, in_specs=[pl.BlockSpec(memory_space=pltpu.VM...]
    all_to_all x2, waiting for transfers between devices: 3.08 us -> 5.47 us  [exchange(): return lax.all_to_all(parts, axes, split_axis=0, concat_axis=0, tiled=True)]
  transfers between devices with their start and end apart: 2 -> 2, of which waited for: 2 -> 2; matrix products, arithmetic and copies ran while one was open for 0% -> 0% of each run, Pallas kernels for 10% -> 7%
where the time goes in v3:
time: 96.9 us; the launch traced here: 96.5 us
  blocking collectives  58.8 us (61%)
  starting transfers between devices  17.8 us (18%)
  Pallas kernels  12.8 us (13%)
  waiting for transfers between devices  5.47 us (6%)
    all_to_all x3, blocking collectives, exchange(): return lax.all_to_all(parts, axes, split_axis=0, concat_axis=0, tiled=True)  58.8 us
    all_to_all x2, starting transfers between devices, exchange(): return lax.all_to_all(parts, axes, split_axis=0, concat_axis=0, tiled=True)  17.8 us
    all_to_all x2, waiting for transfers between devices, exchange(): return lax.all_to_all(parts, axes, split_axis=0, concat_axis=0, tiled=True)  5.47 us
    pallas_call x1, Pallas kernels, count_rows(): pl.pallas_call(count_kernel, in_specs=[pl.BlockSpec(memory_space=pltpu.VM...  5.25 us
    pallas_call x1, Pallas kernels, layer(): pl.pallas_call(layer_kernel, in_specs=[pl.BlockSpec(memory_space=pltpu.SM...  2.97 us
    pallas_call x1, Pallas kernels, select_rows(): pl.pallas_call(select_kernel, out_shape=jax.ShapeDtypeStruct((peers, slot...  2.71 us
  transfers between devices with their start and end apart: 2, of which 2 were waited for; matrix products, arithmetic and copies ran while one was open for 0% of the time, Pallas kernels for 7%

profile of v3, /device:TPU:1, one launch (start us, length us, event | category | flops | bytes accessed | tf_op | source)
XLA Modules:
  0.0 96.5 jit_solution(17751795546781572801)
XLA Ops:
  0.6 13.7 %all-to-all-start = ((s32[8,1,96]{2,1,0:T(1,128)}), s32[8,1,96]{2,1,0:T(1,128)S(1)}, u32[]{:S(2)}, u32[]{:S(2)}) async-start(s32[8,1,96]{2,1,0:T(1,128)} %bitcast.13), calls=%async_computation | async-start | bytes 8192 | tf_op jit(solution)/shard_map/all_to_all | solution.py:287
  14.4 1.9 %prepare.1 = (s32[15,1024]{1,0:T(8,128)S(1)}, bf16[4096,256]{1,0:T(8,128)(2,1)S(1)}) custom-call(s32[15,1024]{1,0:T(8,128)} %bitcast.11, bf16[4096,256]{1,0:T(8,128)(2,1)} %code_hbm.1, bf16[2,4096]{1,0:T(2,128)(2,1)} %bitcast.12), custom_call_target="tpu_custom_call" | custom-call | flops 2097152 | bytes 4194304 | tf_op jit(solution)/shard_map/prepare/pallas_call | solution.py:223
  16.3 2.6 %all-to-all-done = s32[8,1,96]{2,1,0:T(1,128)S(1)} async-done(((s32[8,1,96]{2,1,0:T(1,128)}), s32[8,1,96]{2,1,0:T(1,128)S(1)}, u32[]{:S(2)}, u32[]{:S(2)}) %all-to-all-start) | async-done | bytes 3104 | tf_op jit(solution)/shard_map/all_to_all | solution.py:287
  18.9 2.7 %select_rows.1 = bf16[8,96,256]{2,1,0:T(8,128)(2,1)} custom-call(s32[8,96]{1,0:T(8,128)S(1)} %bitcast.10, bf16[4096,256]{1,0:T(8,128)(2,1)S(1)} %get-tuple-element.14.table_ref), custom_call_target="tpu_custom_call" | custom-call | flops 1610612736 | bytes 3145728 | tf_op jit(solution)/shard_map/select_rows/pallas_call | solution.py:246
  21.6 4.1 %all-to-all-start.1 = ((bf16[8,96,256]{2,1,0:T(8,128)(2,1)}), bf16[8,96,256]{2,1,0:T(8,128)(2,1)S(1)}, u32[]{:S(2)}, u32[]{:S(2)}) async-start(bf16[8,96,256]{2,1,0:T(8,128)(2,1)} %select_rows.1), calls=%async_computation.1 | async-start | bytes 786432 | tf_op jit(solution)/shard_map/all_to_all | solution.py:287
  25.6 0.0 copy-start
  25.7 5.3 %count_rows.1 = (f32[256,1024]{1,0:T(8,128)S(1)}, s32[128,1024]{1,0:T(8,128)S(1)}, bf16[1536,256]{1,0:T(8,128)(2,1)S(1)}, bf16[1024,256]{1,0:T(8,128)(2,1)S(1)}) custom-call(s32[15,1024]{1,0:T(8,128)S(1)} %get-tuple-element.11.nbr_ref, bf16[2048,256]{1,0:T(8,128)(2,1)} %hot_hbm.1, bf16[1024,256]{1,0:T(8,128)(2,1)} %self_hbm.1, bf16[1024,256]{1,0:T(8,128)(2,1)} %grad_hbm.1, ...), custom_call_target="tpu_custom_call" | custom-call | flops 1073741824 | bytes 16777216 | tf_op jit(solution)/shard_map/count_rows/pallas_call | solution.py:195
  30.9 2.8 %all-to-all-done.1.rows_ref = bf16[8,96,256]{2,1,0:T(8,128)(2,1)S(1)} async-done(((bf16[8,96,256]{2,1,0:T(8,128)(2,1)}), bf16[8,96,256]{2,1,0:T(8,128)(2,1)S(1)}, u32[]{:S(2)}, u32[]{:S(2)}) %all-to-all-start.1) | async-done | bytes 393248 | tf_op jit(solution)/shard_map/all_to_all | solution.py:287
  33.7 0.0 copy-done
  33.7 3.0 %layer.1 = (bf16[1024,256]{1,0:T(8,128)(2,1)}, bf16[512,256]{1,0:T(8,128)(2,1)S(1)}) custom-call(s32[8]{0:T(128)S(1)} %copy-done, f32[256,1024]{1,0:T(8,128)S(1)} %get-tuple-element.12.sum_ref, s32[128,1024]{1,0:T(8,128)S(1)} %get-tuple-element.13.words_ref, bf16[8,96,256]{2,1,0:T(8,128)(2,1)S(1)} %all-to-all-done.1.rows_ref, ...), custom_call_target="tpu_custom_call" | custom-call | flops 939524096 | bytes 5242880 | tf_op jit(solution)/shard_map/layer/pallas_call | solution.py:263
  36.7 17.4 %all_to_all.31 = bf16[64,8,256]{2,1,0:T(8,128)(2,1)S(1)} all-to-all(bf16[64,8,256]{2,1,0:T(8,128)(2,1)S(1)} %bitcast.9), channel_id=1, replica_groups=mesh['grp'=8,'own'=8,'rep'=12] {'grp','own'}, dimensions={0} | all-to-all | bytes 524288 | tf_op jit(solution)/shard_map/all_to_all | solution.py:287
  54.1 0.1 convert_reduce_fusion
  54.2 21.8 %all_to_all.32 = f32[12,8,256]{2,1,0:T(8,128)S(1)} all-to-all(f32[12,8,256]{2,1,0:T(8,128)S(1)} %broadcast_in_dim.4), channel_id=1, replica_groups=mesh['grp'=8,'own'=8,'rep'=12] {'rep'}, dimensions={0} | all-to-all | bytes 196608 | tf_op jit(solution)/shard_map/all_to_all | solution.py:287
  76.1 19.6 %all_to_all.33 = bf16[64,8,256]{2,1,0:T(8,128)(2,1)S(1)} all-to-all(bf16[64,8,256]{2,1,0:T(8,128)(2,1)S(1)} %broadcast_in_dim.5), channel_id=1, replica_groups=mesh['grp'=8,'own'=8,'rep'=12] {'grp','own'}, dimensions={0} | all-to-all | bytes 524288 | tf_op jit(solution)/shard_map/all_to_all | solution.py:287
  95.7 0.8 slice_bitcast_fusion
  (4 shorter events, 0.1 us)
Async XLA Ops:
  0.6 18.3 %all-to-all-start = ((s32[8,1,96]{2,1,0:T(1,128)}), s32[8,1,96]{2,1,0:T(1,128)S(1)}, u32[]{:S(2)}, u32[]{:S(2)}) async-start(s32[8,1,96]{2,1,0:T(1,128)} %bitcast.13), calls=%async_computation | async-start | bytes 8192 | tf_op jit(solution)/shard_map/all_to_all | solution.py:287
  21.6 12.2 %all-to-all-start.1 = ((bf16[8,96,256]{2,1,0:T(8,128)(2,1)}), bf16[8,96,256]{2,1,0:T(8,128)(2,1)S(1)}, u32[]{:S(2)}, u32[]{:S(2)}) async-start(bf16[8,96,256]{2,1,0:T(8,128)(2,1)} %select_rows.1), calls=%async_computation.1 | async-start | bytes 786432 | tf_op jit(solution)/shard_map/all_to_all | solution.py:287
  25.6 8.1 %copy-start = (s32[8]{0:T(128)S(1)}, s32[8]{0:T(128)}, u32[]{:S(2)}) copy-start(s32[8]{0:T(128)} %live_ref.1) | copy-start | bytes 100

commit v4 on v3

--- a/solution.py
+++ b/solution.py
@@ -293,9 +293,9 @@
     peers = lax.axis_size("grp") * lax.axis_size("own")
     depth = lax.axis_size("rep")
     parts = exchange(grads.reshape(peers, rows // peers, width), plane)
-    share = jnp.sum(parts.astype(F32), axis=0)
+    share = jnp.sum(parts.astype(F32), axis=0).astype(BF16)
     shares = exchange(jnp.broadcast_to(share[None], (depth,) + share.shape), "rep")
-    share = jnp.sum(shares, axis=0).astype(BF16)
+    share = jnp.sum(shares.astype(F32), axis=0).astype(BF16)
     parts = exchange(jnp.broadcast_to(share[None], (peers,) + share.shape), plane)
     return parts.reshape(rows, width).astype(F32)
 

time: 96.9 us -> 95.7 us (0.988)
  blocking collectives: 58.8 us -> 57.6 us
    all_to_all x3, blocking collectives: 58.8 us -> 57.6 us  [exchange(): return lax.all_to_all(parts, axes, split_axis=0, concat_axis=0, tiled=True)]
where the time goes in v4:
time: 95.7 us; the launch traced here: 95.3 us
  blocking collectives  57.6 us (60%)
  starting transfers between devices  17.8 us (19%)
  Pallas kernels  12.8 us (13%)
  waiting for transfers between devices  5.47 us (6%)
    all_to_all x3, blocking collectives, exchange(): return lax.all_to_all(parts, axes, split_axis=0, concat_axis=0, tiled=True)  57.6 us
    all_to_all x2, starting transfers between devices, exchange(): return lax.all_to_all(parts, axes, split_axis=0, concat_axis=0, tiled=True)  17.8 us
    all_to_all x2, waiting for transfers between devices, exchange(): return lax.all_to_all(parts, axes, split_axis=0, concat_axis=0, tiled=True)  5.47 us
    pallas_call x1, Pallas kernels, count_rows(): pl.pallas_call(count_kernel, in_specs=[pl.BlockSpec(memory_space=pltpu.VM...  5.25 us
    pallas_call x1, Pallas kernels, layer(): pl.pallas_call(layer_kernel, in_specs=[pl.BlockSpec(memory_space=pltpu.SM...  2.97 us
    pallas_call x1, Pallas kernels, select_rows(): pl.pallas_call(select_kernel, out_shape=jax.ShapeDtypeStruct((peers, slot...  2.71 us
  transfers between devices with their start and end apart: 2, of which 2 were waited for; matrix products, arithmetic and copies ran while one was open for 0% of the time, Pallas kernels for 7%

profile of v4, /device:TPU:1, one launch (start us, length us, event | category | flops | bytes accessed | tf_op | source)
XLA Modules:
  0.0 95.3 jit_solution(11889903208863616483)
XLA Ops:
  0.6 13.7 %all-to-all-start = ((s32[8,1,96]{2,1,0:T(1,128)}), s32[8,1,96]{2,1,0:T(1,128)S(1)}, u32[]{:S(2)}, u32[]{:S(2)}) async-start(s32[8,1,96]{2,1,0:T(1,128)} %bitcast.13), calls=%async_computation | async-start | bytes 8192 | tf_op jit(solution)/shard_map/all_to_all | solution.py:287
  14.4 1.9 %prepare.1 = (s32[15,1024]{1,0:T(8,128)S(1)}, bf16[4096,256]{1,0:T(8,128)(2,1)S(1)}) custom-call(s32[15,1024]{1,0:T(8,128)} %bitcast.11, bf16[4096,256]{1,0:T(8,128)(2,1)} %code_hbm.1, bf16[2,4096]{1,0:T(2,128)(2,1)} %bitcast.12), custom_call_target="tpu_custom_call" | custom-call | flops 2097152 | bytes 4194304 | tf_op jit(solution)/shard_map/prepare/pallas_call | solution.py:223
  16.3 2.6 %all-to-all-done = s32[8,1,96]{2,1,0:T(1,128)S(1)} async-done(((s32[8,1,96]{2,1,0:T(1,128)}), s32[8,1,96]{2,1,0:T(1,128)S(1)}, u32[]{:S(2)}, u32[]{:S(2)}) %all-to-all-start) | async-done | bytes 3104 | tf_op jit(solution)/shard_map/all_to_all | solution.py:287
  18.9 2.7 %select_rows.1 = bf16[8,96,256]{2,1,0:T(8,128)(2,1)} custom-call(s32[8,96]{1,0:T(8,128)S(1)} %bitcast.10, bf16[4096,256]{1,0:T(8,128)(2,1)S(1)} %get-tuple-element.14.table_ref), custom_call_target="tpu_custom_call" | custom-call | flops 1610612736 | bytes 3145728 | tf_op jit(solution)/shard_map/select_rows/pallas_call | solution.py:246
  21.6 4.1 %all-to-all-start.1 = ((bf16[8,96,256]{2,1,0:T(8,128)(2,1)}), bf16[8,96,256]{2,1,0:T(8,128)(2,1)S(1)}, u32[]{:S(2)}, u32[]{:S(2)}) async-start(bf16[8,96,256]{2,1,0:T(8,128)(2,1)} %select_rows.1), calls=%async_computation.1 | async-start | bytes 786432 | tf_op jit(solution)/shard_map/all_to_all | solution.py:287
  25.6 0.0 copy-start
  25.7 5.3 %count_rows.1 = (f32[256,1024]{1,0:T(8,128)S(1)}, s32[128,1024]{1,0:T(8,128)S(1)}, bf16[1536,256]{1,0:T(8,128)(2,1)S(1)}, bf16[1024,256]{1,0:T(8,128)(2,1)S(1)}) custom-call(s32[15,1024]{1,0:T(8,128)S(1)} %get-tuple-element.11.nbr_ref, bf16[2048,256]{1,0:T(8,128)(2,1)} %hot_hbm.1, bf16[1024,256]{1,0:T(8,128)(2,1)} %self_hbm.1, bf16[1024,256]{1,0:T(8,128)(2,1)} %grad_hbm.1, ...), custom_call_target="tpu_custom_call" | custom-call | flops 1073741824 | bytes 16777216 | tf_op jit(solution)/shard_map/count_rows/pallas_call | solution.py:195
  30.9 2.8 %all-to-all-done.1.rows_ref = bf16[8,96,256]{2,1,0:T(8,128)(2,1)S(1)} async-done(((bf16[8,96,256]{2,1,0:T(8,128)(2,1)}), bf16[8,96,256]{2,1,0:T(8,128)(2,1)S(1)}, u32[]{:S(2)}, u32[]{:S(2)}) %all-to-all-start.1) | async-done | bytes 393248 | tf_op jit(solution)/shard_map/all_to_all | solution.py:287
  33.7 0.0 copy-done
  33.7 3.0 %layer.1 = (bf16[1024,256]{1,0:T(8,128)(2,1)}, bf16[512,256]{1,0:T(8,128)(2,1)S(1)}) custom-call(s32[8]{0:T(128)S(1)} %copy-done, f32[256,1024]{1,0:T(8,128)S(1)} %get-tuple-element.12.sum_ref, s32[128,1024]{1,0:T(8,128)S(1)} %get-tuple-element.13.words_ref, bf16[8,96,256]{2,1,0:T(8,128)(2,1)S(1)} %all-to-all-done.1.rows_ref, ...), custom_call_target="tpu_custom_call" | custom-call | flops 939524096 | bytes 5242880 | tf_op jit(solution)/shard_map/layer/pallas_call | solution.py:263
  36.7 17.4 %all_to_all.31 = bf16[64,8,256]{2,1,0:T(8,128)(2,1)S(1)} all-to-all(bf16[64,8,256]{2,1,0:T(8,128)(2,1)S(1)} %bitcast.9), channel_id=1, replica_groups=mesh['grp'=8,'own'=8,'rep'=12] {'grp','own'}, dimensions={0} | all-to-all | bytes 524288 | tf_op jit(solution)/shard_map/all_to_all | solution.py:287
  54.1 0.1 reduce_sum.24
  54.2 21.0 %all_to_all.32 = bf16[12,8,256]{2,1,0:T(8,128)(2,1)S(1)} all-to-all(bf16[12,8,256]{2,1,0:T(8,128)(2,1)S(1)} %broadcast_in_dim.4), channel_id=1, replica_groups=mesh['grp'=8,'own'=8,'rep'=12] {'rep'}, dimensions={0} | all-to-all | bytes 98304 | tf_op jit(solution)/shard_map/all_to_all | solution.py:287
  75.3 19.2 %all_to_all.33 = bf16[64,8,256]{2,1,0:T(8,128)(2,1)S(1)} all-to-all(bf16[64,8,256]{2,1,0:T(8,128)(2,1)S(1)} %broadcast_in_dim.5), channel_id=1, replica_groups=mesh['grp'=8,'own'=8,'rep'=12] {'grp','own'}, dimensions={0} | all-to-all | bytes 524288 | tf_op jit(solution)/shard_map/all_to_all | solution.py:287
  94.5 0.8 slice_bitcast_fusion
  (4 shorter events, 0.1 us)
Async XLA Ops:
  0.6 18.3 %all-to-all-start = ((s32[8,1,96]{2,1,0:T(1,128)}), s32[8,1,96]{2,1,0:T(1,128)S(1)}, u32[]{:S(2)}, u32[]{:S(2)}) async-start(s32[8,1,96]{2,1,0:T(1,128)} %bitcast.13), calls=%async_computation | async-start | bytes 8192 | tf_op jit(solution)/shard_map/all_to_all | solution.py:287
  21.6 12.2 %all-to-all-start.1 = ((bf16[8,96,256]{2,1,0:T(8,128)(2,1)}), bf16[8,96,256]{2,1,0:T(8,128)(2,1)S(1)}, u32[]{:S(2)}, u32[]{:S(2)}) async-start(bf16[8,96,256]{2,1,0:T(8,128)(2,1)} %select_rows.1), calls=%async_computation.1 | async-start | bytes 786432 | tf_op jit(solution)/shard_map/all_to_all | solution.py:287
  25.6 8.1 %copy-start = (s32[8]{0:T(128)S(1)}, s32[8]{0:T(128)}, u32[]{:S(2)}) copy-start(s32[8]{0:T(128)} %live_ref.1) | copy-start | bytes 100

commit v5 on v4

--- a/solution.py
+++ b/solution.py
@@ -11,6 +11,7 @@
 STEP = 32
 PEERS = 4
 PARTS = 4
+CHUNKS = 2
 VMEM = 32 * 2**20
 
 
@@ -138,7 +139,7 @@
     grads_ref,
     cold_ref,
     hidden_ref,
-    sem,
+    sems,
 ):
     owners, slots, width = rows_ref.shape
     targets = sum_ref.shape[1]
@@ -146,7 +147,7 @@
     for p in range(owners):
         slot = lax.broadcasted_iota(jnp.int32, (slots, width), 0)
         rows.append(jnp.where(slot < live_ref[p], rows_ref[p].astype(F32), 0.0))
-    cold_ref[:width, :] = jnp.concatenate(rows, axis=0).T.astype(BF16)
+    cold_ref[:width, :] = jnp.concatenate(rows, axis=0).astype(BF16).T
     dead = [
         jnp.where(lax.broadcasted_iota(jnp.int32, (1, slots), 1) < live_ref[p], 0.0, 1.0)
         for p in range(owners)
@@ -154,29 +155,36 @@
     dead = jnp.broadcast_to(jnp.concatenate(dead, axis=1), (STEP, owners * slots))
     cold_ref[width:, :] = dead.astype(BF16)
 
-    words = words_ref[...]
     blocks = owners * slots // LANES
-    counts = jnp.concatenate([counter(words, b) for b in range(blocks)], axis=0)
-    cold = jnp.dot(cold_ref[...], counts, preferred_element_type=F32)
-    share = 1.0 / (16.0 - cold[width : width + 1, :])
-    mean_t = ((sum_ref[...] + cold[:width, :]) * share).astype(BF16)
-    mean = mean_t.T
-    own = held_ref[:targets, :]
-    pre = jnp.dot(own, held_ref[targets : targets + width, :], preferred_element_type=F32) + jnp.dot(
-        mean, held_ref[targets + width :, :], preferred_element_type=F32
-    )
-    sigma = 1.0 / (1.0 + jnp.exp(-pre))
-    hidden_ref[...] = (pre * sigma).astype(BF16)
-    out = pltpu.make_async_copy(hidden_ref, hidden_hbm, sem)
-    out.start()
-    slope = sigma * (1.0 + pre * (1.0 - sigma))
-    delta = (grad_ref[...].astype(F32) * slope).astype(BF16)
-    across = (((0,), (0,)), ((), ()))
-    grads_ref[:width, :] = lax.dot_general(
-        own, delta, across, preferred_element_type=F32
-    ).astype(BF16)
-    grads_ref[width:, :] = jnp.dot(mean_t, delta, preferred_element_type=F32).astype(BF16)
-    out.wait()
+    part = targets // CHUNKS
+    outs = []
+    own_sum = mean_sum = None
+    for i in range(CHUNKS):
+        cut = slice(i * part, (i + 1) * part)
+        words = words_ref[:, cut]
+        counts = jnp.concatenate([counter(words, b) for b in range(blocks)], axis=0)
+        cold = jnp.dot(cold_ref[...], counts, preferred_element_type=F32)
+        share = 1.0 / (16.0 - cold[width : width + 1, :])
+        mean_t = ((sum_ref[:, cut] + cold[:width, :]) * share).astype(BF16)
+        mean = mean_t.T
+        own = held_ref[cut, :]
+        both = jnp.concatenate([own, mean], axis=1)
+        pre = jnp.dot(both, held_ref[targets:, :], preferred_element_type=F32)
+        sigma = 1.0 / (1.0 + jnp.exp(-pre))
+        hidden_ref[cut, :] = (pre * sigma).astype(BF16)
+        outs.append(pltpu.make_async_copy(hidden_ref.at[cut], hidden_hbm.at[cut], sems.at[i]))
+        outs[-1].start()
+        slope = sigma * (1.0 + pre * (1.0 - sigma))
+        delta = (grad_ref[cut, :].astype(F32) * slope).astype(BF16)
+        across = (((0,), (0,)), ((), ()))
+        own_part = lax.dot_general(own, delta, across, preferred_element_type=F32)
+        mean_part = jnp.dot(mean_t, delta, preferred_element_type=F32)
+        own_sum = own_part if i == 0 else own_sum + own_part
+        mean_sum = mean_part if i == 0 else mean_sum + mean_part
+    grads_ref[:width, :] = own_sum.astype(BF16)
+    grads_ref[width:, :] = mean_sum.astype(BF16)
+    for out in outs:
+        out.wait()
 
 
 def outside(array):
@@ -271,7 +279,7 @@
         scratch_shapes=[
             pltpu.VMEM((width + STEP, cold), BF16),
             pltpu.VMEM((targets, width), BF16),
-            pltpu.SemaphoreType.DMA,
+            pltpu.SemaphoreType.DMA((CHUNKS,)),
         ],
         cost_estimate=pl.CostEstimate(
             flops=2 * targets * width * (cold + 4 * width),

time: 95.7 us -> 95.5 us (level)
  no operation moved by 1% of the time
where the time goes in v5:
time: 95.5 us; the launch traced here: 95.1 us
  blocking collectives  57.6 us (60%)
  starting transfers between devices  17.8 us (19%)
  Pallas kernels  12.6 us (13%)
  waiting for transfers between devices  5.47 us (6%)
    all_to_all x3, blocking collectives, exchange(): return lax.all_to_all(parts, axes, split_axis=0, concat_axis=0, tiled=True)  57.6 us
    all_to_all x2, starting transfers between devices, exchange(): return lax.all_to_all(parts, axes, split_axis=0, concat_axis=0, tiled=True)  17.8 us
    all_to_all x2, waiting for transfers between devices, exchange(): return lax.all_to_all(parts, axes, split_axis=0, concat_axis=0, tiled=True)  5.47 us
    pallas_call x1, Pallas kernels, count_rows(): pl.pallas_call(count_kernel, in_specs=[pl.BlockSpec(memory_space=pltpu.VM...  5.25 us
    pallas_call x1, Pallas kernels, layer(): pl.pallas_call(layer_kernel, in_specs=[pl.BlockSpec(memory_space=pltpu.SM...  2.75 us
    pallas_call x1, Pallas kernels, select_rows(): pl.pallas_call(select_kernel, out_shape=jax.ShapeDtypeStruct((peers, slot...  2.71 us
  transfers between devices with their start and end apart: 2, of which 2 were waited for; matrix products, arithmetic and copies ran while one was open for 0% of the time, Pallas kernels for 7%

profile of v5, /device:TPU:1, one launch (start us, length us, event | category | flops | bytes accessed | tf_op | source)
XLA Modules:
  0.0 95.1 jit_solution(14258225747951294594)
XLA Ops:
  0.6 13.7 %all-to-all-start = ((s32[8,1,96]{2,1,0:T(1,128)}), s32[8,1,96]{2,1,0:T(1,128)S(1)}, u32[]{:S(2)}, u32[]{:S(2)}) async-start(s32[8,1,96]{2,1,0:T(1,128)} %bitcast.13), calls=%async_computation | async-start | bytes 8192 | tf_op jit(solution)/shard_map/all_to_all | solution.py:295
  14.4 1.9 %prepare.1 = (s32[15,1024]{1,0:T(8,128)S(1)}, bf16[4096,256]{1,0:T(8,128)(2,1)S(1)}) custom-call(s32[15,1024]{1,0:T(8,128)} %bitcast.11, bf16[4096,256]{1,0:T(8,128)(2,1)} %code_hbm.1, bf16[2,4096]{1,0:T(2,128)(2,1)} %bitcast.12), custom_call_target="tpu_custom_call" | custom-call | flops 2097152 | bytes 4194304 | tf_op jit(solution)/shard_map/prepare/pallas_call | solution.py:231
  16.3 2.6 %all-to-all-done = s32[8,1,96]{2,1,0:T(1,128)S(1)} async-done(((s32[8,1,96]{2,1,0:T(1,128)}), s32[8,1,96]{2,1,0:T(1,128)S(1)}, u32[]{:S(2)}, u32[]{:S(2)}) %all-to-all-start) | async-done | bytes 3104 | tf_op jit(solution)/shard_map/all_to_all | solution.py:295
  18.9 2.7 %select_rows.1 = bf16[8,96,256]{2,1,0:T(8,128)(2,1)} custom-call(s32[8,96]{1,0:T(8,128)S(1)} %bitcast.10, bf16[4096,256]{1,0:T(8,128)(2,1)S(1)} %get-tuple-element.14.table_ref), custom_call_target="tpu_custom_call" | custom-call | flops 1610612736 | bytes 3145728 | tf_op jit(solution)/shard_map/select_rows/pallas_call | solution.py:254
  21.6 4.1 %all-to-all-start.1 = ((bf16[8,96,256]{2,1,0:T(8,128)(2,1)}), bf16[8,96,256]{2,1,0:T(8,128)(2,1)S(1)}, u32[]{:S(2)}, u32[]{:S(2)}) async-start(bf16[8,96,256]{2,1,0:T(8,128)(2,1)} %select_rows.1), calls=%async_computation.1 | async-start | bytes 786432 | tf_op jit(solution)/shard_map/all_to_all | solution.py:295
  25.6 0.0 copy-start
  25.7 5.3 %count_rows.1 = (f32[256,1024]{1,0:T(8,128)S(1)}, s32[128,1024]{1,0:T(8,128)S(1)}, bf16[1536,256]{1,0:T(8,128)(2,1)S(1)}, bf16[1024,256]{1,0:T(8,128)(2,1)S(1)}) custom-call(s32[15,1024]{1,0:T(8,128)S(1)} %get-tuple-element.11.nbr_ref, bf16[2048,256]{1,0:T(8,128)(2,1)} %hot_hbm.1, bf16[1024,256]{1,0:T(8,128)(2,1)} %self_hbm.1, bf16[1024,256]{1,0:T(8,128)(2,1)} %grad_hbm.1, ...), custom_call_target="tpu_custom_call" | custom-call | flops 1073741824 | bytes 16777216 | tf_op jit(solution)/shard_map/count_rows/pallas_call | solution.py:203
  30.9 2.8 %all-to-all-done.1.rows_ref = bf16[8,96,256]{2,1,0:T(8,128)(2,1)S(1)} async-done(((bf16[8,96,256]{2,1,0:T(8,128)(2,1)}), bf16[8,96,256]{2,1,0:T(8,128)(2,1)S(1)}, u32[]{:S(2)}, u32[]{:S(2)}) %all-to-all-start.1) | async-done | bytes 393248 | tf_op jit(solution)/shard_map/all_to_all | solution.py:295
  33.7 0.0 copy-done
  33.7 2.7 %layer.1 = (bf16[1024,256]{1,0:T(8,128)(2,1)}, bf16[512,256]{1,0:T(8,128)(2,1)S(1)}) custom-call(s32[8]{0:T(128)S(1)} %copy-done, f32[256,1024]{1,0:T(8,128)S(1)} %get-tuple-element.12.sum_ref, s32[128,1024]{1,0:T(8,128)S(1)} %get-tuple-element.13.words_ref, bf16[8,96,256]{2,1,0:T(8,128)(2,1)S(1)} %all-to-all-done.1.rows_ref, ...), custom_call_target="tpu_custom_call" | custom-call | flops 939524096 | bytes 5242880 | tf_op jit(solution)/shard_map/layer/pallas_call | solution.py:271
  36.5 17.4 %all_to_all.31 = bf16[64,8,256]{2,1,0:T(8,128)(2,1)S(1)} all-to-all(bf16[64,8,256]{2,1,0:T(8,128)(2,1)S(1)} %bitcast.9), channel_id=1, replica_groups=mesh['grp'=8,'own'=8,'rep'=12] {'grp','own'}, dimensions={0} | all-to-all | bytes 524288 | tf_op jit(solution)/shard_map/all_to_all | solution.py:295
  53.9 0.1 reduce_sum.24
  54.0 21.0 %all_to_all.32 = bf16[12,8,256]{2,1,0:T(8,128)(2,1)S(1)} all-to-all(bf16[12,8,256]{2,1,0:T(8,128)(2,1)S(1)} %broadcast_in_dim.4), channel_id=1, replica_groups=mesh['grp'=8,'own'=8,'rep'=12] {'rep'}, dimensions={0} | all-to-all | bytes 98304 | tf_op jit(solution)/shard_map/all_to_all | solution.py:295
  75.0 19.2 %all_to_all.33 = bf16[64,8,256]{2,1,0:T(8,128)(2,1)S(1)} all-to-all(bf16[64,8,256]{2,1,0:T(8,128)(2,1)S(1)} %broadcast_in_dim.5), channel_id=1, replica_groups=mesh['grp'=8,'own'=8,'rep'=12] {'grp','own'}, dimensions={0} | all-to-all | bytes 524288 | tf_op jit(solution)/shard_map/all_to_all | solution.py:295
  94.3 0.8 slice_bitcast_fusion
  (4 shorter events, 0.1 us)
Async XLA Ops:
  0.6 18.3 %all-to-all-start = ((s32[8,1,96]{2,1,0:T(1,128)}), s32[8,1,96]{2,1,0:T(1,128)S(1)}, u32[]{:S(2)}, u32[]{:S(2)}) async-start(s32[8,1,96]{2,1,0:T(1,128)} %bitcast.13), calls=%async_computation | async-start | bytes 8192 | tf_op jit(solution)/shard_map/all_to_all | solution.py:295
  21.6 12.2 %all-to-all-start.1 = ((bf16[8,96,256]{2,1,0:T(8,128)(2,1)}), bf16[8,96,256]{2,1,0:T(8,128)(2,1)S(1)}, u32[]{:S(2)}, u32[]{:S(2)}) async-start(bf16[8,96,256]{2,1,0:T(8,128)(2,1)} %select_rows.1), calls=%async_computation.1 | async-start | bytes 786432 | tf_op jit(solution)/shard_map/all_to_all | solution.py:295
  25.6 8.1 %copy-start = (s32[8]{0:T(128)S(1)}, s32[8]{0:T(128)}, u32[]{:S(2)}) copy-start(s32[8]{0:T(128)} %live_ref.1) | copy-start | bytes 100

commit v6 on v5

--- a/solution.py
+++ b/solution.py
@@ -170,7 +170,7 @@
         own = held_ref[cut, :]
         both = jnp.concatenate([own, mean], axis=1)
         pre = jnp.dot(both, held_ref[targets:, :], preferred_element_type=F32)
-        sigma = 1.0 / (1.0 + jnp.exp(-pre))
+        sigma = 0.5 + 0.5 * jnp.tanh(0.5 * pre)
         hidden_ref[cut, :] = (pre * sigma).astype(BF16)
         outs.append(pltpu.make_async_copy(hidden_ref.at[cut], hidden_hbm.at[cut], sems.at[i]))
         outs[-1].start()

time: 95.5 us -> 95.5 us (level)
  no operation moved by 1% of the time
where the time goes in v6:
time: 95.5 us; the launch traced here: 95.1 us
  blocking collectives  57.6 us (60%)
  starting transfers between devices  17.8 us (19%)
  Pallas kernels  12.5 us (13%)
  waiting for transfers between devices  5.47 us (6%)
    all_to_all x3, blocking collectives, exchange(): return lax.all_to_all(parts, axes, split_axis=0, concat_axis=0, tiled=True)  57.6 us
    all_to_all x2, starting transfers between devices, exchange(): return lax.all_to_all(parts, axes, split_axis=0, concat_axis=0, tiled=True)  17.8 us
    all_to_all x2, waiting for transfers between devices, exchange(): return lax.all_to_all(parts, axes, split_axis=0, concat_axis=0, tiled=True)  5.47 us
    pallas_call x1, Pallas kernels, count_rows(): pl.pallas_call(count_kernel, in_specs=[pl.BlockSpec(memory_space=pltpu.VM...  5.25 us
    pallas_call x1, Pallas kernels, layer(): pl.pallas_call(layer_kernel, in_specs=[pl.BlockSpec(memory_space=pltpu.SM...  2.71 us
    pallas_call x1, Pallas kernels, select_rows(): pl.pallas_call(select_kernel, out_shape=jax.ShapeDtypeStruct((peers, slot...  2.71 us
  transfers between devices with their start and end apart: 2, of which 2 were waited for; matrix products, arithmetic and copies ran while one was open for 0% of the time, Pallas kernels for 7%

profile of v6, /device:TPU:1, one launch (start us, length us, event | category | flops | bytes accessed | tf_op | source)
XLA Modules:
  0.0 95.1 jit_solution(15895905156080532065)
XLA Ops:
  0.6 13.7 %all-to-all-start = ((s32[8,1,96]{2,1,0:T(1,128)}), s32[8,1,96]{2,1,0:T(1,128)S(1)}, u32[]{:S(2)}, u32[]{:S(2)}) async-start(s32[8,1,96]{2,1,0:T(1,128)} %bitcast.13), calls=%async_computation | async-start | bytes 8192 | tf_op jit(solution)/shard_map/all_to_all | solution.py:295
  14.4 1.9 %prepare.1 = (s32[15,1024]{1,0:T(8,128)S(1)}, bf16[4096,256]{1,0:T(8,128)(2,1)S(1)}) custom-call(s32[15,1024]{1,0:T(8,128)} %bitcast.11, bf16[4096,256]{1,0:T(8,128)(2,1)} %code_hbm.1, bf16[2,4096]{1,0:T(2,128)(2,1)} %bitcast.12), custom_call_target="tpu_custom_call" | custom-call | flops 2097152 | bytes 4194304 | tf_op jit(solution)/shard_map/prepare/pallas_call | solution.py:231
  16.3 2.6 %all-to-all-done = s32[8,1,96]{2,1,0:T(1,128)S(1)} async-done(((s32[8,1,96]{2,1,0:T(1,128)}), s32[8,1,96]{2,1,0:T(1,128)S(1)}, u32[]{:S(2)}, u32[]{:S(2)}) %all-to-all-start) | async-done | bytes 3104 | tf_op jit(solution)/shard_map/all_to_all | solution.py:295
  18.9 2.7 %select_rows.1 = bf16[8,96,256]{2,1,0:T(8,128)(2,1)} custom-call(s32[8,96]{1,0:T(8,128)S(1)} %bitcast.10, bf16[4096,256]{1,0:T(8,128)(2,1)S(1)} %get-tuple-element.14.table_ref), custom_call_target="tpu_custom_call" | custom-call | flops 1610612736 | bytes 3145728 | tf_op jit(solution)/shard_map/select_rows/pallas_call | solution.py:254
  21.6 4.1 %all-to-all-start.1 = ((bf16[8,96,256]{2,1,0:T(8,128)(2,1)}), bf16[8,96,256]{2,1,0:T(8,128)(2,1)S(1)}, u32[]{:S(2)}, u32[]{:S(2)}) async-start(bf16[8,96,256]{2,1,0:T(8,128)(2,1)} %select_rows.1), calls=%async_computation.1 | async-start | bytes 786432 | tf_op jit(solution)/shard_map/all_to_all | solution.py:295
  25.6 0.0 copy-start
  25.7 5.3 %count_rows.1 = (f32[256,1024]{1,0:T(8,128)S(1)}, s32[128,1024]{1,0:T(8,128)S(1)}, bf16[1536,256]{1,0:T(8,128)(2,1)S(1)}, bf16[1024,256]{1,0:T(8,128)(2,1)S(1)}) custom-call(s32[15,1024]{1,0:T(8,128)S(1)} %get-tuple-element.11.nbr_ref, bf16[2048,256]{1,0:T(8,128)(2,1)} %hot_hbm.1, bf16[1024,256]{1,0:T(8,128)(2,1)} %self_hbm.1, bf16[1024,256]{1,0:T(8,128)(2,1)} %grad_hbm.1, ...), custom_call_target="tpu_custom_call" | custom-call | flops 1073741824 | bytes 16777216 | tf_op jit(solution)/shard_map/count_rows/pallas_call | solution.py:203
  30.9 2.8 %all-to-all-done.1.rows_ref = bf16[8,96,256]{2,1,0:T(8,128)(2,1)S(1)} async-done(((bf16[8,96,256]{2,1,0:T(8,128)(2,1)}), bf16[8,96,256]{2,1,0:T(8,128)(2,1)S(1)}, u32[]{:S(2)}, u32[]{:S(2)}) %all-to-all-start.1) | async-done | bytes 393248 | tf_op jit(solution)/shard_map/all_to_all | solution.py:295
  33.7 0.0 copy-done
  33.7 2.7 %layer.1 = (bf16[1024,256]{1,0:T(8,128)(2,1)}, bf16[512,256]{1,0:T(8,128)(2,1)S(1)}) custom-call(s32[8]{0:T(128)S(1)} %copy-done, f32[256,1024]{1,0:T(8,128)S(1)} %get-tuple-element.12.sum_ref, s32[128,1024]{1,0:T(8,128)S(1)} %get-tuple-element.13.words_ref, bf16[8,96,256]{2,1,0:T(8,128)(2,1)S(1)} %all-to-all-done.1.rows_ref, ...), custom_call_target="tpu_custom_call" | custom-call | flops 939524096 | bytes 5242880 | tf_op jit(solution)/shard_map/layer/pallas_call | solution.py:271
  36.5 17.4 %all_to_all.31 = bf16[64,8,256]{2,1,0:T(8,128)(2,1)S(1)} all-to-all(bf16[64,8,256]{2,1,0:T(8,128)(2,1)S(1)} %bitcast.9), channel_id=1, replica_groups=mesh['grp'=8,'own'=8,'rep'=12] {'grp','own'}, dimensions={0} | all-to-all | bytes 524288 | tf_op jit(solution)/shard_map/all_to_all | solution.py:295
  53.8 0.1 reduce_sum.24
  53.9 21.0 %all_to_all.32 = bf16[12,8,256]{2,1,0:T(8,128)(2,1)S(1)} all-to-all(bf16[12,8,256]{2,1,0:T(8,128)(2,1)S(1)} %broadcast_in_dim.4), channel_id=1, replica_groups=mesh['grp'=8,'own'=8,'rep'=12] {'rep'}, dimensions={0} | all-to-all | bytes 98304 | tf_op jit(solution)/shard_map/all_to_all | solution.py:295
  75.0 19.2 %all_to_all.33 = bf16[64,8,256]{2,1,0:T(8,128)(2,1)S(1)} all-to-all(bf16[64,8,256]{2,1,0:T(8,128)(2,1)S(1)} %broadcast_in_dim.5), channel_id=1, replica_groups=mesh['grp'=8,'own'=8,'rep'=12] {'grp','own'}, dimensions={0} | all-to-all | bytes 524288 | tf_op jit(solution)/shard_map/all_to_all | solution.py:295
  94.2 0.8 slice_bitcast_fusion
  (4 shorter events, 0.1 us)
Async XLA Ops:
  0.6 18.3 %all-to-all-start = ((s32[8,1,96]{2,1,0:T(1,128)}), s32[8,1,96]{2,1,0:T(1,128)S(1)}, u32[]{:S(2)}, u32[]{:S(2)}) async-start(s32[8,1,96]{2,1,0:T(1,128)} %bitcast.13), calls=%async_computation | async-start | bytes 8192 | tf_op jit(solution)/shard_map/all_to_all | solution.py:295
  21.6 12.2 %all-to-all-start.1 = ((bf16[8,96,256]{2,1,0:T(8,128)(2,1)}), bf16[8,96,256]{2,1,0:T(8,128)(2,1)S(1)}, u32[]{:S(2)}, u32[]{:S(2)}) async-start(bf16[8,96,256]{2,1,0:T(8,128)(2,1)} %select_rows.1), calls=%async_computation.1 | async-start | bytes 786432 | tf_op jit(solution)/shard_map/all_to_all | solution.py:295
  25.6 8.1 %copy-start = (s32[8]{0:T(128)S(1)}, s32[8]{0:T(128)}, u32[]{:S(2)}) copy-start(s32[8]{0:T(128)} %live_ref.1) | copy-start | bytes 100
